TPU v7x, 1024 devices: a whole 4x4x32 slice. The times are simulated.
1024 devices in a mesh: pipe: 16 (over z_lo, core), expert: 64 (over y, z_hi, x).
Axes of the slice: x: 4, y: 4, z: 32 (z_hi: 4, z_lo: 8; z = z_hi * 8 + z_lo), core: 2. Of those that a mesh axis runs over, the one named last changes fastest.
Arguments:
- forward_rows: bfloat16 [16, 32, 7168], P('pipe', None, 'expert'), may hold values from -6 to 6
- backward_rows: bfloat16 [16, 32, 7168], P('pipe', None, 'expert'), may hold values from -6 to 6
- route_ids: int32 [2, 2, 16, 32, 2], P(None, None, 'pipe'), may hold values from 0 to 3, all different within a row
- norm_gain: float32 [16, 7168], P('pipe'), may hold values from 0.1 to 1.9
- router_weight: float32 [16, 4, 7168], P('pipe'), may hold values from -0.0625 to 0.0625
- w_gate_up: bfloat16 [16, 7168, 8192], P('pipe', None, 'expert'), may hold values from -0.0625 to 0.0625
- w_down: bfloat16 [16, 4096, 7168], P('pipe', None, 'expert'), may hold values from -0.09375 to 0.09375
Outputs:
- forward_out: bfloat16 [16, 32, 7168], P('pipe', None, 'expert')
- backward_out: bfloat16 [16, 32, 7168], P('pipe', None, 'expert')
Inputs may be any that keep to these rules, and one draw needn't show every extreme that they name: `route_ids`: each token names 2 different experts.
All inputs are finite; a program needn't handle non-finite values.
Results may differ from a plain program's by a relative error of at most 0.0075.
Values may be sent and summed in bfloat16 or wider, within the bound.
No kernel may reach another device: no remote copies, remote signals or barrier semaphores. Data moves between devices by JAX's collectives and lax.ppermute only.
A program may use at most 32 MiB of HBM per device.

v0:
```python
import jax
import jax.numpy as jnp
from jax import lax
from jax.sharding import PartitionSpec as P

FF = 1024
EXPERTS = 4


EPSILON = 1e-06
ROUTE_SCALE = 2.5


def passed_along(block, axis, distance):
    devices = range(lax.axis_size(axis))
    route = [(i - distance, i) for i in devices if i - distance in devices]
    return lax.ppermute(block, axis, route)


def hidden_units(full_rows, chosen_ids, gain_row, router_mat, packed_in, unit_expert):
    widened = full_rows.astype(jnp.float32)
    mean_square = jnp.mean(widened * widened, axis=-1, keepdims=True)
    normed = (widened * lax.rsqrt(mean_square + EPSILON) * gain_row).astype(jnp.bfloat16)
    logits = lax.dot_general(
        normed.astype(jnp.float32),
        router_mat,
        (((1,), (1,)), ((), ())),
        precision=lax.Precision.HIGHEST,
    )
    scores = jax.nn.sigmoid(logits)
    picked = jnp.take_along_axis(scores, chosen_ids, axis=1)
    gate_share = picked / jnp.sum(picked, axis=1, keepdims=True)
    expert_range = jnp.arange(EXPERTS, dtype=jnp.int32)
    chosen = (chosen_ids[:, :, None] == expert_range[None, None, :]).astype(jnp.float32)
    route_weight = ROUTE_SCALE * jnp.sum(chosen * gate_share[:, :, None], axis=1)
    owner = (unit_expert[None, :] == expert_range[:, None]).astype(jnp.float32)
    unit_weight = jnp.dot(route_weight, owner, precision=lax.Precision.HIGHEST)
    projected = jnp.dot(normed, packed_in, preferred_element_type=jnp.float32)
    unit_count = projected.shape[1] // 2
    gate_part = projected[:, :unit_count]
    up_part = projected[:, unit_count:]
    return (jax.nn.silu(gate_part) * up_part * unit_weight).astype(jnp.bfloat16)


def shards(forward_rows, backward_rows, route_ids, norm_gain, router_weight, w_gate_up, w_down):
    gain_row = norm_gain[0]
    router_mat = router_weight[0]
    packed_in = w_gate_up[0]
    down_mat = w_down[0]
    unit_count = packed_in.shape[1] // 2
    unit_expert = (
        lax.axis_index("expert") * unit_count + jnp.arange(unit_count, dtype=jnp.int32)
    ) // FF
    share_width = forward_rows.shape[2]
    offset = lax.axis_index("expert") * share_width
    batch_rows = forward_rows.shape[1]
    steps_total = route_ids.shape[0]

    def gather_rows(row_pair):
        return (
            lax.all_gather(row_pair[0], "expert", axis=1, tiled=True),
            lax.all_gather(row_pair[1], "expert", axis=1, tiled=True),
        )

    shares = (forward_rows[0], backward_rows[0])
    full_pair = gather_rows(shares)
    for moment in range(steps_total):
        stacked = jnp.concatenate([full_pair[0], full_pair[1]], axis=0)
        stacked_ids = jnp.concatenate([route_ids[moment, 0, 0], route_ids[moment, 1, 0]], axis=0)
        layer_hidden_both = hidden_units(
            stacked, stacked_ids, gain_row, router_mat, packed_in, unit_expert
        )
        updates = jnp.dot(
            lax.all_gather(layer_hidden_both, "expert", axis=1, tiled=True),
            down_mat,
            preferred_element_type=jnp.float32,
        )
        first_out = (shares[0].astype(jnp.float32) + updates[:batch_rows]).astype(jnp.bfloat16)
        second_out = (shares[1].astype(jnp.float32) + updates[batch_rows:]).astype(jnp.bfloat16)
        shares = (first_out, second_out)
        if moment + 1 < steps_total:
            assembled = gather_rows(shares)
            moved_forward = passed_along(assembled[0], "pipe", 1)
            moved_backward = passed_along(assembled[1], "pipe", -1)
            full_pair = (moved_forward, moved_backward)
            shares = (
                lax.dynamic_slice_in_dim(moved_forward, offset, share_width, 1),
                lax.dynamic_slice_in_dim(moved_backward, offset, share_width, 1),
            )
    return (shares[0][None], shares[1][None])


def solution(mesh):
    return jax.shard_map(
        shards,
        mesh=mesh,
        in_specs=(
            P("pipe", None, "expert"),
            P("pipe", None, "expert"),
            P(None, None, "pipe", None, None),
            P("pipe", None),
            P("pipe", None, None),
            P("pipe", None, "expert"),
            P("pipe", None, "expert"),
        ),
        out_specs=(P("pipe", None, "expert"), P("pipe", None, "expert")),
        check_vma=False,
    )
```

profile of v0, /device:TPU:32, one launch (start us, length us, event | category | flops | bytes accessed | tf_op | source)
XLA Modules:
  0.0 2137.6 jit_solution(17364581249004326)
XLA Ops:
  0.6 0.0 copy-start
  0.6 0.9 copy.45
  1.6 466.2 %all-gather.1 = bf16[1,32,7168]{1,0,2:T(2,128)(2,1)} all-gather(bf16[1,32,112]{1,0,2:T(2,128)(2,1)S(1)} %copy.45), channel_id=3, replica_groups=mesh['pipe'=16,'expert'=64] {'expert'}, dimensions={2}, use_global_device_ids=true | all-gather | bytes 465920 | tf_op jit(solution)/shard_map/all_gather | solution.py:62
  467.8 0.0 copy-start.3
  467.8 7.0 copy.46
  474.8 0.0 copy-done.3
  474.8 0.1 copy.43
  474.9 438.1 %all-gather = bf16[1,32,7168]{1,0,2:T(2,128)(2,1)} all-gather(bf16[1,32,112]{1,0,2:T(2,128)(2,1)S(1)} %copy.43), channel_id=2, replica_groups=mesh['pipe'=16,'expert'=64] {'expert'}, dimensions={2}, use_global_device_ids=true | all-gather | bytes 465920 | tf_op jit(solution)/shard_map/all_gather | solution.py:61
  913.1 0.0 copy-start.6
  913.1 7.0 copy.44
  920.1 0.3 fusion
  920.4 0.0 copy-done
  920.4 0.0 copy-done.6
  920.4 0.0 copy-start.5
  920.4 0.5 fusion.8
  920.9 0.4 copy-done.5
  921.3 0.0 copy-start.4
  921.3 0.9 fusion.17
  922.2 0.0 copy-done.4
  922.2 0.1 bitcast_or_fusion
  922.3 0.1 copy.47
  922.4 0.1 reshape.85
  922.5 0.0 copy-start.1
  922.6 1.5 gather_fusion
  924.1 0.0 copy-start.2
  924.1 0.1 reshape.88
  924.2 0.1 copy.48
  924.4 0.2 fusion.10
  924.6 0.1 copy.49
  924.7 297.7 %all_gather.20 = bf16[64,4096]{0,1:T(8,128)(2,1)S(1)} all-gather(bf16[64,64]{0,1:T(8,128)(2,1)S(1)} %copy.49), channel_id=1, replica_groups=mesh['pipe'=16,'expert'=64] {'expert'}, dimensions={1}, use_global_device_ids=true | all-gather | bytes 532480 | tf_op jit(solution)/shard_map/all_gather | solution.py:74
  1222.4 0.0 copy-done.1
  1222.4 0.4 fusion.20
  1222.8 0.0 copy-done.2
  1222.8 294.2 %all-gather.3 = bf16[64,112,32]{1,2,0:T(8,128)(2,1)S(1)} all-gather(bf16[1,112,32]{1,2,0:T(8,128)(2,1)S(1)} %get-tuple-element.14), channel_id=1, replica_groups=mesh['pipe'=16,'expert'=64] {'expert'}, dimensions={0}, use_global_device_ids=true | all-gather | bytes 465920 | tf_op jit(solution)/shard_map/all_gather | solution.py:62
  1517.0 0.2 copy.51
  1517.2 1.7 reshape.83
  1519.0 1.9 collective-permute-start.1
  1520.9 297.6 %all-gather.2 = bf16[64,112,32]{1,2,0:T(8,128)(2,1)S(1)} all-gather(bf16[1,112,32]{1,2,0:T(8,128)(2,1)S(1)} %get-tuple-element.13), channel_id=1, replica_groups=mesh['pipe'=16,'expert'=64] {'expert'}, dimensions={0}, use_global_device_ids=true | all-gather | bytes 465920 | tf_op jit(solution)/shard_map/all_gather | solution.py:61
  1818.5 0.2 copy.50
  1818.7 1.7 reshape.81
  1820.4 1.9 collective-permute-start
  1822.3 0.1 copy.52
  1822.4 0.1 reshape.90
  1822.6 0.0 collective-permute-done.1
  1822.6 7.8 collective-permute-done
  1830.4 1.3 fusion.3
  1831.7 1.9 fusion.14
  1833.6 1.5 gather_fusion.1
  1835.2 0.1 reshape.93
  1835.3 0.1 copy.53
  1835.4 1.5 fusion.6
  1836.9 0.2 fusion.11
  1837.2 0.1 copy.54
  1837.3 298.5 %all_gather.23 = bf16[64,4096]{0,1:T(8,128)(2,1)S(1)} all-gather(bf16[64,64]{0,1:T(8,128)(2,1)S(1)} %copy.54), channel_id=1, replica_groups=mesh['pipe'=16,'expert'=64] {'expert'}, dimensions={1}, use_global_device_ids=true | all-gather | bytes 532480 | tf_op jit(solution)/shard_map/all_gather | solution.py:74
  2135.8 0.4 fusion.18
  2136.2 1.4 fusion.31
  (11 shorter events, 0.1 us)
Async XLA Ops:
  0.6 919.7 %copy-start = (bf16[1,7168,128]{2,1,0:T(8,128)(2,1)S(1)}, bf16[1,7168,128]{2,1,0:T(8,128)(2,1)}, u32[]{:S(2)}) copy-start(bf16[1,7168,128]{2,1,0:T(8,128)(2,1)} %param.14) | copy-start | bytes 5505028
  467.8 7.0 copy-start.3
  913.1 7.3 copy-start.6
  920.4 0.9 copy-start.5
  921.3 0.9 copy-start.4
  922.5 299.8 %copy-start.1 = (bf16[1,4096,112]{1,2,0:T(8,128)(2,1)S(1)}, bf16[1,4096,112]{1,2,0:T(8,128)(2,1)}, u32[]{:S(2)}) copy-start(bf16[1,4096,112]{1,2,0:T(8,128)(2,1)} %param.15) | copy-start | bytes 2752516
  924.1 298.7 %copy-start.2 = (bf16[1,32,112]{2,1,0:T(8,128)(2,1)S(1)}, bf16[1,32,112]{2,1,0:T(8,128)(2,1)}, u32[]{:S(2)}) copy-start(bf16[1,32,112]{2,1,0:T(8,128)(2,1)} %param.10) | copy-start | bytes 21508
  1519.0 303.6 %collective-permute-start.1 = (bf16[32,7168]{1,0:T(8,128)(2,1)}, bf16[32,7168]{1,0:T(8,128)(2,1)}, u32[]{:S(2)}, u32[]{:S(2)}) collective-permute-start(bf16[32,7168]{1,0:T(8,128)(2,1)} %bitcast.66), channel_id=1, source_target_pairs={{64,0},{128,64},{192,128},{256,192},{320,256},{384,320},{448,384},... | collective-permute-start | bytes 1376264 | tf_op jit(solution)/shard_map/ppermute | solution.py:17
  1820.4 10.0 collective-permute-start
where the time goes:
time: 2140 us
  blocking collectives  2090 us (98%)
  local copies, waits for them, and re-layouts  23.5 us (1%)
    all_gather x2, blocking collectives, gather_rows(): lax.all_gather(row_pair[1], 'expert', axis=1, tiled=True)  760 us
    all_gather x2, blocking collectives, gather_rows(): lax.all_gather(row_pair[0], 'expert', axis=1, tiled=True)  736 us
    all_gather x2, blocking collectives, shards(): lax.all_gather(layer_hidden_both, 'expert', axis=1, tiled=True)  596 us
  transfers between devices with their start and end apart: 2, of which 1 were waited for; matrix products, arithmetic and copies ran while one was open for 0% of the time, Pallas kernels for 0%

commit v1 on v0

v1 whole, which is shorter than its diff:
```python
import jax
import jax.numpy as jnp
from jax import lax
from jax.sharding import Mesh, PartitionSpec as P

EPSILON = 1e-06
ROUTE_SCALE = 2.5
PLANE = ("y", "x")


def passed_along(block, axis, distance):
    devices = range(lax.axis_size(axis))
    route = [(i - distance, i) for i in devices if i - distance in devices]
    return lax.ppermute(block, axis, route)


def everyone(block, axes):
    size = lax.axis_size(axes)
    return lax.all_to_all(jnp.broadcast_to(block[None], (size, *block.shape)), axes, 0, 0)


def gathered(tile):
    full = everyone(everyone(tile, "zh"), PLANE)
    return full.reshape(-1, tile.shape[1])


def by_plane(array, rows):
    y, zh, x = (lax.axis_size(a) for a in ("y", "zh", "x"))
    split = array.reshape(y, zh, x, 2, rows // 2, array.shape[1])
    return split.transpose(0, 2, 1, 4, 3, 5).reshape(-1, 2, array.shape[1])


def folded(columns):
    half = columns.shape[0] // 2
    return jnp.concatenate([columns[:half], columns[half:]], axis=1)


def unfolded(tile):
    lanes = tile.shape[1] // 2
    return jnp.concatenate([tile[:, :lanes], tile[:, lanes:]], axis=0)


def diagonal(product, rows, lanes):
    return product[:rows, :lanes] + product[rows:, lanes:]


def bf16_pieces(value):
    pieces = []
    for _ in range(3):
        piece = lax.reduce_precision(value, 8, 7)
        pieces.append(piece.astype(jnp.bfloat16))
        value = value - piece
    return pieces


def shards(forward_rows, backward_rows, route_ids, norm_gain, router_weight, w_gate_up, w_down):
    packed_in = w_gate_up[0]
    down_mat = w_down[0]
    share = forward_rows.shape[2]
    batch = forward_rows.shape[1]
    tokens = 2 * batch
    width = packed_in.shape[0]
    columns = packed_in.shape[1]
    units = columns // 2
    experts = router_weight.shape[1]
    steps_total = route_ids.shape[0]
    own_expert = lax.axis_index(("y", "zh", "x")) * units // (down_mat.shape[0] // experts)

    gain = norm_gain[0][:, None]
    scaled_in = (packed_in.astype(jnp.float32) * gain).astype(jnp.bfloat16)
    in_t = by_plane(scaled_in, share).reshape(width // 2, 2 * columns).T
    router_cols = by_plane(router_weight[0].T * gain, share)
    router_cols = router_cols.reshape(width // 2, 2 * experts)
    router_t = jnp.concatenate(bf16_pieces(router_cols.T), axis=0)
    in_t = jnp.concatenate([in_t, router_t], axis=0)
    down_t = by_plane(down_mat, units).reshape(down_mat.shape[0] // 2, 2 * share).T

    lane = lax.broadcasted_iota(jnp.int32, (1, 2 * tokens), 1)
    is_forward = lane % tokens < batch
    state = jnp.concatenate([forward_rows[0], backward_rows[0]], axis=0).T
    tile = folded(state)
    for moment in range(steps_total):
        rows = gathered(tile)
        wide = rows.astype(jnp.float32)
        squares = jnp.sum(wide * wide, axis=0, keepdims=True)
        mean_square = (squares[:, :tokens] + squares[:, tokens:]) / width
        inverse = lax.rsqrt(mean_square + EPSILON)
        product = jnp.dot(in_t, rows, preferred_element_type=jnp.float32)
        projected = diagonal(product[: 2 * columns], columns, tokens) * inverse
        routed = product[2 * columns :].reshape(3, 2 * experts, 2 * tokens).sum(0)
        scores = jax.nn.sigmoid(diagonal(routed, experts, tokens) * inverse)
        ids = jnp.concatenate([route_ids[moment, 0, 0], route_ids[moment, 1, 0]], axis=0).T
        named = lax.broadcasted_iota(jnp.int32, (experts, 1), 0)[:, None] == ids[None]
        picked = jnp.sum(jnp.where(named, scores[:, None], 0.0), axis=0)
        total = jnp.sum(picked, axis=0, keepdims=True)
        mine = jnp.sum(jnp.where(ids == own_expert, picked, 0.0), axis=0, keepdims=True)
        weight = ROUTE_SCALE * (mine / total)
        hidden = jax.nn.silu(projected[:units]) * projected[units:] * weight
        everything = gathered(folded(hidden.astype(jnp.bfloat16)))
        update = jnp.dot(down_t, everything, preferred_element_type=jnp.float32)
        state = state.astype(jnp.float32) + diagonal(update, share, tokens)
        state = state.astype(jnp.bfloat16)
        if moment + 1 < steps_total:
            tile = folded(state)
            tile = jnp.where(
                is_forward, passed_along(tile, "pipe", 1), passed_along(tile, "pipe", -1)
            )
            state = unfolded(tile)
    final = state.T
    return (final[None, :batch], final[None, batch:])


def solution(mesh):
    fine = Mesh(mesh.devices.reshape(-1, 4, 4, 4), ("pipe", "y", "zh", "x"))
    expert = ("y", "zh", "x")
    return jax.shard_map(
        shards,
        mesh=fine,
        in_specs=(
            P("pipe", None, expert),
            P("pipe", None, expert),
            P(None, None, "pipe", None, None),
            P("pipe", None),
            P("pipe", None, None),
            P("pipe", None, expert),
            P("pipe", None, expert),
        ),
        out_specs=(P("pipe", None, expert), P("pipe", None, expert)),
        check_vma=False,
    )
```

time: 2140 us -> 231 us (0.11)
  blocking collectives: 2090 us -> 107 us
  starting transfers between devices: 3.82 us -> 47.2 us
  waiting for transfers between devices: 7.83 us -> 35.9 us
    all_gather x6 -> x0, blocking collectives: 2090 us -> none  [the longest x2 760 us: gather_rows(): lax.all_gather(row_pair[1], 'expert', axis=1, tiled=True)]
    all_to_all x0 -> x4, blocking collectives: none -> 107 us  [everyone(): lax.all_to_all(jnp.broadcast_to(block[None], (size, *block.shape)), axes,...]
    all_to_all x0 -> x4, starting transfers between devices: none -> 41.7 us  [everyone(): lax.all_to_all(jnp.broadcast_to(block[None], (size, *block.shape)), axes,...]
    all_to_all x0 -> x4, waiting for transfers between devices: none -> 34.5 us  [everyone(): lax.all_to_all(jnp.broadcast_to(block[None], (size, *block.shape)), axes,...]
  transfers between devices with their start and end apart: 2 -> 6, of which waited for: 1 -> 5; matrix products, arithmetic and copies ran while one was open for 0% -> 10% of each run, Pallas kernels for 0% -> 0%
where the time goes in v1:
time: 231 us; the launch traced here: 230 us
  blocking collectives  107 us (46%)
  starting transfers between devices  47.2 us (20%)
  waiting for transfers between devices  35.9 us (16%)
  local copies, waits for them, and re-layouts  23.5 us (10%)
  other arithmetic  9.9 us (4%)
  matrix products  5.26 us (2%)
    all_to_all x4, blocking collectives, everyone(): lax.all_to_all(jnp.broadcast_to(block[None], (size, *block.shape)), axes,...  107 us
    all_to_all x4, starting transfers between devices, everyone(): lax.all_to_all(jnp.broadcast_to(block[None], (size, *block.shape)), axes,...  41.7 us
    all_to_all x4, waiting for transfers between devices, everyone(): lax.all_to_all(jnp.broadcast_to(block[None], (size, *block.shape)), axes,...  34.5 us
    unnamed x15, local copies, waits for them, and re-layouts  7.4 us
    ppermute x2, starting transfers between devices, passed_along(): return lax.ppermute(block, axis, route)  5.55 us
    transpose x2, local copies, waits for them, and re-layouts, by_plane(): return split.transpose(0, 2, 1, 4, 3, 5).reshape(-1, 2, array.shape[1])  5.07 us
  transfers between devices with their start and end apart: 6, of which 5 were waited for; matrix products, arithmetic and copies ran while one was open for 10% of the time, Pallas kernels for 0%

profile of v1, /device:TPU:32, one launch (start us, length us, event | category | flops | bytes accessed | tf_op | source)
XLA Modules:
  0.0 229.7 jit_solution(9970223505681401773)
XLA Ops:
  0.6 0.0 copy-start.2
  0.7 0.9 copy.34
  1.6 0.8 copy.33
  2.4 0.1 maximum_bitcast_fusion
  2.5 0.1 pad_maximum_fusion.1
  2.6 0.6 broadcast_in_dim.56
  3.2 27.4 %all-to-all-start = ((bf16[4,56,128]{2,1,0:T(8,128)(2,1)}), bf16[4,56,128]{2,1,0:T(8,128)(2,1)S(1)}, u32[]{:S(2)}, u32[]{:S(2)}) async-start(bf16[4,56,128]{2,1,0:T(8,128)(2,1)} %broadcast_in_dim.56), calls=%async_computation | async-start | bytes 114688 | tf_op jit(solution)/shard_map/all_to_all | solution.py:19
  30.7 0.9 fusion.4
  31.6 0.5 reshape.80
  32.1 0.1 copy.48
  32.2 0.2 reshape_reshape.10
  32.5 1.2 copy.39
  33.7 1.3 copy.38
  35.0 1.2 copy.37
  36.2 0.5 broadcast.88
  36.7 0.7 reduce.7
  37.4 0.1 mul.122
  37.6 1.1 fusion.1
  38.7 1.7 copy.35
  40.5 1.5 copy.47
  42.0 13.9 %all-to-all-done = bf16[4,56,128]{2,1,0:T(8,128)(2,1)S(1)} async-done(((bf16[4,56,128]{2,1,0:T(8,128)(2,1)}), bf16[4,56,128]{2,1,0:T(8,128)(2,1)S(1)}, u32[]{:S(2)}, u32[]{:S(2)}) %all-to-all-start) | async-done | bytes 57376 | tf_op jit(solution)/shard_map/all_to_all | solution.py:19
  55.9 1.1 broadcast_in_dim.57
  57.0 7.1 %all-to-all-start.1 = ((bf16[16,4,56,128]{3,2,1,0:T(8,128)(2,1)}), bf16[16,4,56,128]{3,2,1,0:T(8,128)(2,1)}, u32[]{:S(2)}, u32[]{:S(2)}) async-start(bf16[16,4,56,128]{3,2,1,0:T(8,128)(2,1)} %broadcast_in_dim.57), calls=%async_computation.1 | async-start | bytes 1835008 | tf_op jit(solution)/shard_map/all_to_all | solution.py:19
  64.1 0.1 add_bitcast_fusion
  64.2 3.6 %pad_maximum_fusion = bf16[280,3584]{0,1:T(8,128)(2,1)S(1)} fusion(bf16[8,3584]{0,1:T(8,128)(2,1)} %copy.39, bf16[8,3584]{0,1:T(8,128)(2,1)} %copy.38, bf16[8,3584]{0,1:T(8,128)(2,1)} %copy.37, bf16[256,3584]{0,1:T(8,128)(2,1)} %bitcast.91), kind=kLoop, calls=%fused_computation.2 | loop fusion | flops 8028160 | bytes 4014080 | tf_op jit(solution)/shard_map/concatenate | solution.py:75
  67.8 8.5 %all-to-all-done.1 = bf16[16,4,56,128]{3,2,1,0:T(8,128)(2,1)} async-done(((bf16[16,4,56,128]{3,2,1,0:T(8,128)(2,1)}), bf16[16,4,56,128]{3,2,1,0:T(8,128)(2,1)}, u32[]{:S(2)}, u32[]{:S(2)}) %all-to-all-start.1) | async-done | bytes 917536 | tf_op jit(solution)/shard_map/all_to_all | solution.py:19
  76.3 1.7 multiply_reduce_fusion.1
  78.0 0.1 rsqrt_bitcast_fusion.1
  78.1 2.1 fusion.26
  80.2 0.1 fusion.6
  80.3 0.1 add_divide_fusion.1
  80.4 0.1 pad_maximum_fusion.3
  80.5 32.9 %all_to_all.40 = bf16[4,32,128]{2,1,0:T(8,128)(2,1)S(1)} all-to-all(bf16[4,32,128]{2,1,0:T(8,128)(2,1)S(1)} %broadcast_in_dim.106), channel_id=1, replica_groups=mesh['pipe'=16,'y'=4,'zh'=4,'x'=4] {'zh'}, dimensions={0} | all-to-all | bytes 65536 | tf_op jit(solution)/shard_map/all_to_all | solution.py:19
  113.5 0.9 broadcast_in_dim.107
  114.4 3.6 %all-to-all-start.3 = ((bf16[16,4,32,128]{3,2,1,0:T(8,128)(2,1)}), bf16[16,4,32,128]{3,2,1,0:T(8,128)(2,1)S(1)}, u32[]{:S(2)}, u32[]{:S(2)}) async-start(bf16[16,4,32,128]{3,2,1,0:T(8,128)(2,1)} %broadcast_in_dim.107), calls=%async_computation.3 | async-start | bytes 1048576 | tf_op jit(solution)/shard_map/all_to_all | solution.py:19
  117.9 2.3 copy.40
  120.2 3.4 %copy.41 = bf16[4,4,4,32,2,112]{5,4,3,2,1,0:T(2,128)(2,1)} copy(bf16[4,4,4,32,2,112]{5,3,4,1,2,0:T(8,128)(2,1)} %bitcast.93) | data formatting | bytes 1835008 | tf_op jit(solution)/shard_map/transpose | solution.py:30
  123.6 2.4 %reshape_reshape.11 = bf16[2048,224]{1,0:T(8,128)(2,1)} reshape(bf16[4,4,4,32,2,112]{5,4,3,2,1,0:T(2,128)(2,1)} %copy.41) | data formatting | bytes 1835008 | tf_op jit(solution)/shard_map/reshape;reshape | solution.py:76
  126.0 2.0 all-to-all-done.3
  128.0 1.7 convolution_bitcast_fusion.1
  129.8 0.1 fusion.10
  129.9 0.1 pad_maximum_fusion.2
  130.0 1.9 collective-permute-start
  131.9 3.6 %collective-permute-start.1 = (bf16[56,128]{1,0:T(8,128)(2,1)S(1)}, bf16[56,128]{1,0:T(8,128)(2,1)S(1)}, u32[]{:S(2)}, u32[]{:S(2)}) collective-permute-start(bf16[56,128]{1,0:T(8,128)(2,1)S(1)} %pad_maximum_fusion.2), channel_id=1, source_target_pairs={{64,0},{128,64},{192,128},{256,192},{320,256},{384,320},{448,384},... | collective-permute-start | bytes 43016 | tf_op jit(solution)/shard_map/ppermute | solution.py:14
  135.6 1.4 collective-permute-done.1
  137.0 25.7 %all_to_all.41 = bf16[4,56,128]{2,1,0:T(8,128)(2,1)S(1)} all-to-all(bf16[4,56,128]{2,1,0:T(8,128)(2,1)S(1)} %broadcast_in_dim.108), channel_id=1, replica_groups=mesh['pipe'=16,'y'=4,'zh'=4,'x'=4] {'zh'}, dimensions={0} | all-to-all | bytes 114688 | tf_op jit(solution)/shard_map/all_to_all | solution.py:19
  162.7 0.1 broadcast_in_dim.109
  162.8 20.9 %all_to_all.42 = bf16[16,4,56,128]{3,2,1,0:T(8,128)(2,1)S(1)} all-to-all(bf16[16,4,56,128]{3,2,1,0:T(8,128)(2,1)S(1)} %broadcast_in_dim.109), channel_id=1, replica_groups=mesh['pipe'=16,'y'=4,'zh'=4,'x'=4] {'y','x'}, dimensions={0} | all-to-all | bytes 1835008 | tf_op jit(solution)/shard_map/all_to_all | solution.py:19
  183.7 0.9 fusion.27
  184.7 0.5 multiply_reduce_fusion
  185.2 0.1 rsqrt_bitcast_fusion
  185.2 0.1 fusion.5
  185.3 0.1 add_divide_fusion
  185.5 0.1 pad_maximum_fusion.4
  185.6 27.4 %all_to_all.43 = bf16[4,32,128]{2,1,0:T(8,128)(2,1)S(1)} all-to-all(bf16[4,32,128]{2,1,0:T(8,128)(2,1)S(1)} %broadcast_in_dim.112), channel_id=1, replica_groups=mesh['pipe'=16,'y'=4,'zh'=4,'x'=4] {'zh'}, dimensions={0} | all-to-all | bytes 65536 | tf_op jit(solution)/shard_map/all_to_all | solution.py:19
  213.0 0.9 broadcast_in_dim.113
  214.0 3.6 %all-to-all-start.7 = ((bf16[16,4,32,128]{3,2,1,0:T(8,128)(2,1)}), bf16[16,4,32,128]{3,2,1,0:T(8,128)(2,1)S(1)}, u32[]{:S(2)}, u32[]{:S(2)}) async-start(bf16[16,4,32,128]{3,2,1,0:T(8,128)(2,1)} %broadcast_in_dim.113), calls=%async_computation.7 | async-start | bytes 1048576 | tf_op jit(solution)/shard_map/all_to_all | solution.py:19
  217.5 0.1 fusion.25
  217.6 10.0 %all-to-all-done.7 = bf16[16,4,32,128]{3,2,1,0:T(8,128)(2,1)S(1)} async-done(((bf16[16,4,32,128]{3,2,1,0:T(8,128)(2,1)}), bf16[16,4,32,128]{3,2,1,0:T(8,128)(2,1)S(1)}, u32[]{:S(2)}, u32[]{:S(2)}) %all-to-all-start.7) | async-done | bytes 524320 | tf_op jit(solution)/shard_map/all_to_all | solution.py:19
  227.6 0.5 convolution_bitcast_fusion
  228.2 0.1 fusion.15
  228.3 0.1 slice_bitcast_fusion
  228.3 0.7 copy.42
  229.0 0.7 copy.43
  (29 shorter events, 0.3 us)
Async XLA Ops:
  0.6 36.1 %copy-start.2 = (f32[1,7168]{1,0:T(1,128)S(1)}, f32[1,7168]{1,0:T(1,128)}, u32[]{:S(2)}) copy-start(f32[1,7168]{1,0:T(1,128)} %param.10) | copy-start | bytes 86020
  0.6 37.0 %copy-start.1 = (bf16[1,7168,128]{2,1,0:T(8,128)(2,1)S(1)}, bf16[1,7168,128]{2,1,0:T(8,128)(2,1)}, u32[]{:S(2)}) copy-start(bf16[1,7168,128]{2,1,0:T(8,128)(2,1)} %param.12) | copy-start | bytes 5505028
  3.2 52.7 %all-to-all-start = ((bf16[4,56,128]{2,1,0:T(8,128)(2,1)}), bf16[4,56,128]{2,1,0:T(8,128)(2,1)S(1)}, u32[]{:S(2)}, u32[]{:S(2)}) async-start(bf16[4,56,128]{2,1,0:T(8,128)(2,1)} %broadcast_in_dim.56), calls=%async_computation | async-start | bytes 114688 | tf_op jit(solution)/shard_map/all_to_all | solution.py:19
  40.5 23.6 %copy-start.3 = (s32[2,2,1,32,2]{3,4,2,1,0:T(2,128)S(1)}, s32[2,2,1,32,2]{3,4,2,1,0:T(2,128)}, u32[]{:S(2)}) copy-start(s32[2,2,1,32,2]{3,4,2,1,0:T(2,128)} %param.9) | copy-start | bytes 3076
  57.0 19.4 %all-to-all-start.1 = ((bf16[16,4,56,128]{3,2,1,0:T(8,128)(2,1)}), bf16[16,4,56,128]{3,2,1,0:T(8,128)(2,1)}, u32[]{:S(2)}, u32[]{:S(2)}) async-start(bf16[16,4,56,128]{3,2,1,0:T(8,128)(2,1)} %broadcast_in_dim.57), calls=%async_computation.1 | async-start | bytes 1835008 | tf_op jit(solution)/shard_map/all_to_all | solution.py:19
  114.4 13.7 %all-to-all-start.3 = ((bf16[16,4,32,128]{3,2,1,0:T(8,128)(2,1)}), bf16[16,4,32,128]{3,2,1,0:T(8,128)(2,1)S(1)}, u32[]{:S(2)}, u32[]{:S(2)}) async-start(bf16[16,4,32,128]{3,2,1,0:T(8,128)(2,1)} %broadcast_in_dim.107), calls=%async_computation.3 | async-start | bytes 1048576 | tf_op jit(solution)/shard_map/all_to_all | solution.py:19
  130.0 5.6 %collective-permute-start = (bf16[56,128]{1,0:T(8,128)(2,1)S(1)}, bf16[56,128]{1,0:T(8,128)(2,1)S(1)}, u32[]{:S(2)}, u32[]{:S(2)}) collective-permute-start(bf16[56,128]{1,0:T(8,128)(2,1)S(1)} %pad_maximum_fusion.2), channel_id=1, source_target_pairs={{0,64},{64,128},{128,192},{192,256},{256,320},{320,384},{384,448},... | collective-permute-start | bytes 43016 | tf_op jit(solution)/shard_map/ppermute | solution.py:14
  131.9 5.1 %collective-permute-start.1 = (bf16[56,128]{1,0:T(8,128)(2,1)S(1)}, bf16[56,128]{1,0:T(8,128)(2,1)S(1)}, u32[]{:S(2)}, u32[]{:S(2)}) collective-permute-start(bf16[56,128]{1,0:T(8,128)(2,1)S(1)} %pad_maximum_fusion.2), channel_id=1, source_target_pairs={{64,0},{128,64},{192,128},{256,192},{320,256},{384,320},{448,384},... | collective-permute-start | bytes 43016 | tf_op jit(solution)/shard_map/ppermute | solution.py:14
  184.7 43.0 %copy-start = (bf16[2048,224]{1,0:T(8,128)(2,1)S(1)}, bf16[2048,224]{1,0:T(8,128)(2,1)}, u32[]{:S(2)}) copy-start(bf16[2048,224]{1,0:T(8,128)(2,1)} %reshape_reshape.11) | copy-start | bytes 2752516
  214.0 13.7 %all-to-all-start.7 = ((bf16[16,4,32,128]{3,2,1,0:T(8,128)(2,1)}), bf16[16,4,32,128]{3,2,1,0:T(8,128)(2,1)S(1)}, u32[]{:S(2)}, u32[]{:S(2)}) async-start(bf16[16,4,32,128]{3,2,1,0:T(8,128)(2,1)} %broadcast_in_dim.113), calls=%async_computation.7 | async-start | bytes 1048576 | tf_op jit(solution)/shard_map/all_to_all | solution.py:19

commit v2 on v0

v2 whole, which is shorter than its diff:
```python
import jax
import jax.numpy as jnp
from jax import lax
from jax.experimental import pallas as pl
from jax.experimental.pallas import tpu as pltpu
from jax.sharding import Mesh, PartitionSpec as P

EPSILON = 1e-06
ROUTE_SCALE = 2.5
PLANE = ("y", "x")
EXPERT = ("y", "zh", "x")
LANES = 128
STATS = 16


def passed_along(block, axis, distance):
    devices = range(lax.axis_size(axis))
    route = [(i - distance, i) for i in devices if i - distance in devices]
    return lax.ppermute(block, axis, route)


def everyone(copies, axes):
    return lax.all_to_all(copies, axes, 0, 0)


def gathered(copies):
    column = everyone(copies, "zh")
    size = lax.axis_size(PLANE)
    full = everyone(jnp.broadcast_to(column[None], (size, *column.shape)), PLANE)
    return full.reshape(-1, *copies.shape[1:])


def lower_lanes(shape):
    return lax.broadcasted_iota(jnp.int32, shape, 1) < LANES // 2


def turned(value):
    return pltpu.roll(value, LANES // 2, 1)


def natural(place, sizes):
    y, zh, x = sizes
    at_y, rest = divmod(place, x * zh)
    at_x, at_zh = divmod(rest, zh)
    return (at_y * zh + at_zh) * x + at_x


def write_tile(rows, coefs, tile_ref):
    scaled = rows * coefs[:, 0:1]
    sums = [jnp.sum(rows * rows, axis=0, keepdims=True)]
    for e in range(1, 5):
        sums.append(jnp.sum(rows * coefs[:, e : e + 1], axis=0, keepdims=True))
    sums.append(jnp.zeros((3, LANES), jnp.float32))
    sums = jnp.concatenate(sums, axis=0)
    high = sums.astype(jnp.bfloat16).astype(jnp.float32)
    upper = jnp.concatenate([scaled[64:], high, sums - high], axis=0)
    tile = jnp.where(lower_lanes((64, LANES)), scaled[:64], turned(upper))
    tile = tile.astype(jnp.bfloat16)
    for copy in range(tile_ref.shape[0]):
        tile_ref[copy] = tile


def enter_kernel(forward_ref, backward_ref, coefs_ref, tile_ref, state_ref):
    f = forward_ref[...].astype(jnp.float32)
    b = backward_ref[...].astype(jnp.float32)
    rows = jnp.concatenate([f, b, f, b], axis=0).T
    state_ref[...] = rows
    write_tile(rows, coefs_ref[...], tile_ref)


def pass_kernel(previous_ref, next_ref, coefs_ref, tile_ref, state_ref):
    lane = lax.broadcasted_iota(jnp.int32, (64, LANES), 1)
    mixed = jnp.where(
        lane % 64 < 32,
        previous_ref[...].astype(jnp.float32),
        next_ref[...].astype(jnp.float32),
    )
    rows = jnp.concatenate([mixed, turned(mixed)[:48]], axis=0)
    state_ref[...] = rows
    write_tile(rows, coefs_ref[...], tile_ref)


def hidden_kernel(sizes, width, own_ref, gathered_ref, weight_ref, ids_ref, out_ref, rows_ref):
    share = weight_ref.shape[1] // gathered_ref.shape[0]
    stats = jnp.zeros((STATS, LANES), jnp.float32)
    for place in range(gathered_ref.shape[0]):
        tile = gathered_ref[place].astype(jnp.float32)
        start = natural(place, sizes) * share
        rows_ref[start : start + 64, :] = gathered_ref[place]
        rows_ref[start + 64 : start + share, :] = turned(tile[:48]).astype(jnp.bfloat16)
        stats = stats + tile[48:]
    stats = turned(stats[:8] + stats[8:])
    inverse = lax.rsqrt(stats[0:1] / width + EPSILON)
    projected = jnp.dot(
        weight_ref[...], rows_ref[...], preferred_element_type=jnp.float32
    ) * inverse
    scores = 1.0 / (1.0 + jnp.exp(-(stats[1:5] * inverse)))
    total = jnp.zeros((1, LANES), jnp.float32)
    mine = jnp.zeros((1, LANES), jnp.float32)
    for k in range(ids_ref.shape[0]):
        ids = ids_ref[k : k + 1, :]
        picked = jnp.zeros((1, LANES), jnp.float32)
        for e in range(4):
            picked = jnp.where(ids == e, scores[e : e + 1], picked)
        total = total + picked
        mine = mine + jnp.where(ids == own_ref[0], picked, 0.0)
    weight = ROUTE_SCALE * (mine / total)
    gate, up = projected[:64], projected[64:]
    hidden = gate / (1.0 + jnp.exp(-gate)) * up * weight
    folded = jnp.where(lower_lanes((32, LANES)), hidden[:32], turned(hidden[32:]))
    folded = folded.astype(jnp.bfloat16)
    for copy in range(out_ref.shape[0]):
        out_ref[copy] = folded


def updated(sizes, gathered_ref, weight_ref, state_ref, rows_ref):
    for place in range(gathered_ref.shape[0]):
        start = natural(place, sizes) * 64
        rows_ref[start : start + 32, :] = gathered_ref[place]
        rows_ref[start + 32 : start + 64, :] = turned(
            gathered_ref[place].astype(jnp.float32)
        ).astype(jnp.bfloat16)
    return state_ref[...] + jnp.dot(
        weight_ref[...], rows_ref[...], preferred_element_type=jnp.float32
    )


def middle_kernel(sizes, gathered_ref, weight_ref, state_ref, out_ref, rows_ref):
    state = updated(sizes, gathered_ref, weight_ref, state_ref, rows_ref)
    upper = jnp.concatenate([state[64:], jnp.zeros((16, LANES), jnp.float32)], axis=0)
    tile = jnp.where(lower_lanes((64, LANES)), state[:64], turned(upper))
    out_ref[...] = tile.astype(jnp.bfloat16)


def last_kernel(sizes, gathered_ref, weight_ref, state_ref, forward_ref, backward_ref, rows_ref):
    state = updated(sizes, gathered_ref, weight_ref, state_ref, rows_ref).T
    forward_ref[...] = state[:32].astype(jnp.bfloat16)
    backward_ref[...] = state[32:64].astype(jnp.bfloat16)


def local(kernel, outs, scratch, flops, *args, scalars=0):
    vmem = pl.BlockSpec(memory_space=pltpu.VMEM)
    smem = pl.BlockSpec(memory_space=pltpu.SMEM)
    moved = sum(a.size * a.dtype.itemsize for a in (*args, *outs))
    return pl.pallas_call(
        kernel,
        out_shape=outs,
        in_specs=[smem] * scalars + [vmem] * (len(args) - scalars),
        out_specs=tuple(vmem for _ in outs),
        scratch_shapes=scratch,
        cost_estimate=pl.CostEstimate(flops=flops, bytes_accessed=moved, transcendentals=0),
        compiler_params=pltpu.CompilerParams(vmem_limit_bytes=16 * 2**20),
    )(*args)


def shards(forward_rows, backward_rows, route_ids, norm_gain, router_weight, w_gate_up, w_down):
    sizes = tuple(lax.axis_size(a) for a in EXPERT)
    share = forward_rows.shape[2]
    width, columns = w_gate_up.shape[1:]
    all_units = w_down.shape[1]
    me = lax.axis_index(EXPERT)
    own = (me * (columns // 2) // (all_units // router_weight.shape[1])).reshape(1)
    steps_total = route_ids.shape[0]
    tile = (64, LANES)
    half = jnp.bfloat16

    gain = lax.dynamic_slice_in_dim(norm_gain, me * share, share, 1)
    router = lax.dynamic_slice_in_dim(router_weight[0], me * share, share, 1)
    coefs = jnp.concatenate([gain, router * gain, jnp.zeros((3, share), jnp.float32)], axis=0).T
    both = route_ids[:, :, 0].transpose(0, 3, 1, 2).reshape(steps_total, 2, -1)
    both = jnp.concatenate([both, both], axis=2)

    entry_outs = (
        jax.ShapeDtypeStruct((sizes[1], *tile), half),
        jax.ShapeDtypeStruct((share, LANES), jnp.float32),
    )
    copies, state = local(
        enter_kernel, entry_outs, [], 0, forward_rows[0], backward_rows[0], coefs
    )
    in_t = w_gate_up[0].T
    down_t = w_down[0].T
    for moment in range(steps_total):
        rows = gathered(copies)
        (hidden,) = local(
            lambda *refs: hidden_kernel(sizes, width, *refs),
            (jax.ShapeDtypeStruct((sizes[1], 32, LANES), half),),
            [pltpu.VMEM((width, LANES), half)],
            2 * width * columns * LANES,
            own,
            rows,
            in_t,
            both[moment],
            scalars=1,
        )
        units = gathered(hidden)
        scratch = [pltpu.VMEM((all_units, LANES), half)]
        flops = 2 * all_units * share * LANES
        if moment + 1 < steps_total:
            (raw,) = local(
                lambda *refs: middle_kernel(sizes, *refs),
                (jax.ShapeDtypeStruct(tile, half),),
                scratch,
                flops,
                units,
                down_t,
                state,
            )
            copies, state = local(
                pass_kernel,
                entry_outs,
                [],
                0,
                passed_along(raw, "pipe", 1),
                passed_along(raw, "pipe", -1),
                coefs,
            )
        else:
            rows_out = jax.ShapeDtypeStruct((forward_rows.shape[1], share), half)
            outs = local(
                lambda *refs: last_kernel(sizes, *refs),
                (rows_out, rows_out),
                scratch,
                flops,
                units,
                down_t,
                state,
            )
    return (outs[0][None], outs[1][None])


def solution(mesh):
    fine = Mesh(mesh.devices.reshape(-1, 4, 4, 4), ("pipe", *EXPERT))
    return jax.shard_map(
        shards,
        mesh=fine,
        in_specs=(
            P("pipe", None, EXPERT),
            P("pipe", None, EXPERT),
            P(None, None, "pipe", None, None),
            P("pipe", None),
            P("pipe", None, None),
            P("pipe", None, EXPERT),
            P("pipe", None, EXPERT),
        ),
        out_specs=(P("pipe", None, EXPERT), P("pipe", None, EXPERT)),
        check_vma=False,
    )
```

time: 2140 us -> 210 us (0.10)
  the two profiles are of different devices: /device:TPU:32 before, /device:TPU:2 now
where the time goes in v2:
time: 210 us; the launch traced here: 209 us
  blocking collectives  172 us (82%)
  waiting for transfers between devices  13 us (6%)
  starting transfers between devices  11.8 us (6%)
  local copies, waits for them, and re-layouts  6.96 us (3%)
  Pallas kernels  3.87 us (2%)
    all_to_all x7, blocking collectives, everyone(): return lax.all_to_all(copies, axes, 0, 0)  172 us
    all_to_all x1, waiting for transfers between devices, everyone(): return lax.all_to_all(copies, axes, 0, 0)  12.1 us
    all_to_all x1, starting transfers between devices, everyone(): return lax.all_to_all(copies, axes, 0, 0)  7.48 us
    unnamed x11, local copies, waits for them, and re-layouts  4.9 us
    ppermute x2, starting transfers between devices, passed_along(): return lax.ppermute(block, axis, route)  4.32 us
  transfers between devices with their start and end apart: 3, of which 2 were waited for; matrix products, arithmetic and copies ran while one was open for 1% of the time, Pallas kernels for 0%

profile of v2, /device:TPU:2, one launch (start us, length us, event | category | flops | bytes accessed | tf_op | source)
XLA Modules:
  0.0 208.8 jit_solution(13961411662564643675)
XLA Ops:
  0.6 0.0 copy-start
  0.6 0.0 copy-start.4
  0.7 0.7 copy-done
  1.4 0.1 fusion.3
  1.5 0.1 constant_dynamic-slice_fusion
  1.5 0.1 pad.4.clone
  1.6 0.8 bitcast_multiply_fusion
  2.4 0.1 maximum_maximum_fusion
  2.4 0.1 copy.17
  2.5 0.0 copy-start.2
  2.5 0.7 copy-done.2
  3.2 0.0 copy-start.3
  3.2 0.7 copy-done.3
  3.9 0.3 shard_map.86
  4.2 50.9 %all_to_all.40 = bf16[4,64,128]{2,1,0:T(8,128)(2,1)S(1)} all-to-all(bf16[4,64,128]{2,1,0:T(8,128)(2,1)S(1)} %get-tuple-element.8), channel_id=1, replica_groups=mesh['pipe'=16,'y'=4,'zh'=4,'x'=4] {'zh'}, dimensions={0} | all-to-all | bytes 131072 | tf_op jit(solution)/shard_map/all_to_all | solution.py:23
  55.1 1.2 broadcast_in_dim.15
  56.3 7.5 %all-to-all-start.1 = ((bf16[16,4,64,128]{3,2,1,0:T(8,128)(2,1)}), bf16[16,4,64,128]{3,2,1,0:T(8,128)(2,1)S(1)}, u32[]{:S(2)}, u32[]{:S(2)}) async-start(bf16[16,4,64,128]{3,2,1,0:T(8,128)(2,1)} %broadcast_in_dim.15), calls=%async_computation.1 | async-start | bytes 2097152 | tf_op jit(solution)/shard_map/all_to_all | solution.py:23
  63.8 0.0 copy-done.4
  63.8 0.1 reshape.29
  63.9 2.8 %copy.18 = bf16[1,7168,128]{1,2,0:T(8,128)(2,1)S(1)} copy(bf16[1,7168,128]{2,1,0:T(8,128)(2,1)} %param.12) | data formatting | bytes 3670016 | tf_op args[5]
  66.7 0.1 fusion.2
  66.8 12.1 %all-to-all-done.1 = bf16[16,4,64,128]{3,2,1,0:T(8,128)(2,1)S(1)} async-done(((bf16[16,4,64,128]{3,2,1,0:T(8,128)(2,1)}), bf16[16,4,64,128]{3,2,1,0:T(8,128)(2,1)S(1)}, u32[]{:S(2)}, u32[]{:S(2)}) %all-to-all-start.1) | async-done | bytes 1048608 | tf_op jit(solution)/shard_map/all_to_all | solution.py:23
  78.9 0.0 copy-start.1
  78.9 0.8 shard_map.87
  79.7 24.6 %all_to_all.41 = bf16[4,32,128]{2,1,0:T(8,128)(2,1)S(1)} all-to-all(bf16[4,32,128]{2,1,0:T(8,128)(2,1)S(1)} %shard_map.87), channel_id=1, replica_groups=mesh['pipe'=16,'y'=4,'zh'=4,'x'=4] {'zh'}, dimensions={0} | all-to-all | bytes 65536 | tf_op jit(solution)/shard_map/all_to_all | solution.py:23
  104.4 0.1 broadcast_in_dim.16
  104.5 13.0 %all_to_all.42 = bf16[16,4,32,128]{3,2,1,0:T(8,128)(2,1)S(1)} all-to-all(bf16[16,4,32,128]{3,2,1,0:T(8,128)(2,1)S(1)} %broadcast_in_dim.16), channel_id=1, replica_groups=mesh['pipe'=16,'y'=4,'zh'=4,'x'=4] {'y','x'}, dimensions={0} | all-to-all | bytes 1048576 | tf_op jit(solution)/shard_map/all_to_all | solution.py:23
  117.5 0.0 copy-done.1
  117.5 0.6 shard_map.88
  118.0 1.3 collective-permute-start.1
  119.3 3.0 %collective-permute-start = (bf16[64,128]{1,0:T(8,128)(2,1)S(1)}, bf16[64,128]{1,0:T(8,128)(2,1)S(1)}, u32[]{:S(2)}, u32[]{:S(2)}) collective-permute-start(bf16[64,128]{1,0:T(8,128)(2,1)S(1)} %shard_map.88), channel_id=1, source_target_pairs={{0,64},{64,128},{128,192},{192,256},{256,320},{320,384},{384,448},... | collective-permute-start | bytes 49160 | tf_op jit(solution)/shard_map/ppermute | solution.py:19
  122.4 0.0 collective-permute-done.1.next_ref
  122.4 0.8 collective-permute-done.previous_ref
  123.2 0.2 shard_map.89
  123.4 25.9 %all_to_all.43 = bf16[4,64,128]{2,1,0:T(8,128)(2,1)S(1)} all-to-all(bf16[4,64,128]{2,1,0:T(8,128)(2,1)S(1)} %get-tuple-element.10), channel_id=1, replica_groups=mesh['pipe'=16,'y'=4,'zh'=4,'x'=4] {'zh'}, dimensions={0} | all-to-all | bytes 131072 | tf_op jit(solution)/shard_map/all_to_all | solution.py:23
  149.3 0.2 broadcast_in_dim.17
  149.5 18.8 %all_to_all.44 = bf16[16,4,64,128]{3,2,1,0:T(8,128)(2,1)S(1)} all-to-all(bf16[16,4,64,128]{3,2,1,0:T(8,128)(2,1)S(1)} %broadcast_in_dim.17), channel_id=1, replica_groups=mesh['pipe'=16,'y'=4,'zh'=4,'x'=4] {'y','x'}, dimensions={0} | all-to-all | bytes 2097152 | tf_op jit(solution)/shard_map/all_to_all | solution.py:23
  168.3 0.8 shard_map.90
  169.1 25.4 %all_to_all.45 = bf16[4,32,128]{2,1,0:T(8,128)(2,1)S(1)} all-to-all(bf16[4,32,128]{2,1,0:T(8,128)(2,1)S(1)} %shard_map.90), channel_id=1, replica_groups=mesh['pipe'=16,'y'=4,'zh'=4,'x'=4] {'zh'}, dimensions={0} | all-to-all | bytes 65536 | tf_op jit(solution)/shard_map/all_to_all | solution.py:23
  194.5 0.1 broadcast_in_dim.18
  194.6 13.1 %all_to_all.46 = bf16[16,4,32,128]{3,2,1,0:T(8,128)(2,1)S(1)} all-to-all(bf16[16,4,32,128]{3,2,1,0:T(8,128)(2,1)S(1)} %broadcast_in_dim.18), channel_id=1, replica_groups=mesh['pipe'=16,'y'=4,'zh'=4,'x'=4] {'y','x'}, dimensions={0} | all-to-all | bytes 1048576 | tf_op jit(solution)/shard_map/all_to_all | solution.py:23
  207.7 1.1 shard_map.91
  (2 shorter events, 0.0 us)
Async XLA Ops:
  0.6 0.8 copy-start
  0.6 63.1 %copy-start.4 = (s32[2,2,1,32,2]{3,4,2,1,0:T(2,128)S(1)}, s32[2,2,1,32,2]{3,4,2,1,0:T(2,128)}, u32[]{:S(2)}) copy-start(s32[2,2,1,32,2]{3,4,2,1,0:T(2,128)} %param.9) | copy-start | bytes 3076
  2.5 0.7 copy-start.2
  3.2 0.7 copy-start.3
  56.3 22.6 %all-to-all-start.1 = ((bf16[16,4,64,128]{3,2,1,0:T(8,128)(2,1)}), bf16[16,4,64,128]{3,2,1,0:T(8,128)(2,1)S(1)}, u32[]{:S(2)}, u32[]{:S(2)}) async-start(bf16[16,4,64,128]{3,2,1,0:T(8,128)(2,1)} %broadcast_in_dim.15), calls=%async_computation.1 | async-start | bytes 2097152 | tf_op jit(solution)/shard_map/all_to_all | solution.py:23
  78.9 38.6 %copy-start.1 = (bf16[1,4096,112]{1,2,0:T(8,128)(2,1)S(1)}, bf16[1,4096,112]{1,2,0:T(8,128)(2,1)}, u32[]{:S(2)}) copy-start(bf16[1,4096,112]{1,2,0:T(8,128)(2,1)} %param.13) | copy-start | bytes 2752516
  118.0 4.3 %collective-permute-start.1 = (bf16[64,128]{1,0:T(8,128)(2,1)S(1)}, bf16[64,128]{1,0:T(8,128)(2,1)S(1)}, u32[]{:S(2)}, u32[]{:S(2)}) collective-permute-start(bf16[64,128]{1,0:T(8,128)(2,1)S(1)} %shard_map.88), channel_id=1, source_target_pairs={{64,0},{128,64},{192,128},{256,192},{320,256},{384,320},{448,384},... | collective-permute-start | bytes 49160 | tf_op jit(solution)/shard_map/ppermute | solution.py:19
  119.3 3.9 %collective-permute-start = (bf16[64,128]{1,0:T(8,128)(2,1)S(1)}, bf16[64,128]{1,0:T(8,128)(2,1)S(1)}, u32[]{:S(2)}, u32[]{:S(2)}) collective-permute-start(bf16[64,128]{1,0:T(8,128)(2,1)S(1)} %shard_map.88), channel_id=1, source_target_pairs={{0,64},{64,128},{128,192},{192,256},{256,320},{320,384},{384,448},... | collective-permute-start | bytes 49160 | tf_op jit(solution)/shard_map/ppermute | solution.py:19

commit v3 on v2

--- a/solution.py
+++ b/solution.py
@@ -11,6 +11,7 @@
 EXPERT = ("y", "zh", "x")
 LANES = 128
 STATS = 16
+VMEM_MIB = 60
 
 
 def passed_along(block, axis, distance):
@@ -23,11 +24,12 @@
     return lax.all_to_all(copies, axes, 0, 0)
 
 
-def gathered(copies):
+def gathered(copies, meanwhile=()):
     column = everyone(copies, "zh")
+    column, meanwhile = lax.optimization_barrier((column, meanwhile))
     size = lax.axis_size(PLANE)
     full = everyone(jnp.broadcast_to(column[None], (size, *column.shape)), PLANE)
-    return full.reshape(-1, *copies.shape[1:])
+    return full.reshape(-1, *copies.shape[1:]), meanwhile
 
 
 def lower_lanes(shape):
@@ -60,12 +62,53 @@
         tile_ref[copy] = tile
 
 
-def enter_kernel(forward_ref, backward_ref, coefs_ref, tile_ref, state_ref):
+def enter_kernel(
+    me_ref,
+    forward_hbm,
+    backward_hbm,
+    gain_hbm,
+    router_hbm,
+    tile_ref,
+    state_ref,
+    coefs_ref,
+    forward_ref,
+    backward_ref,
+    gain_ref,
+    router_ref,
+    arrived,
+):
+    pairs = (
+        (gain_hbm, gain_ref),
+        (router_hbm, router_ref),
+        (forward_hbm, forward_ref),
+        (backward_hbm, backward_ref),
+    )
+    fetches = [
+        pltpu.make_async_copy(source, target, arrived.at[i])
+        for i, (source, target) in enumerate(pairs)
+    ]
+    for fetch in fetches:
+        fetch.start()
+    for fetch in fetches:
+        fetch.wait()
+    share = forward_ref.shape[1]
+    window = 2 * LANES
+    start = me_ref[0] * share
+    last = gain_ref.shape[1] // LANES - 2
+    base = pl.multiple_of(jnp.minimum(start // LANES, last) * LANES, LANES)
+    gain = gain_ref[:, pl.ds(base, window)]
+    router = router_ref[:, pl.ds(base, window)]
+    coefs = jnp.concatenate(
+        [gain, router * gain, jnp.zeros((3, window), jnp.float32)], axis=0
+    )
+    coefs = pltpu.roll(coefs, lax.rem(window - (start - base), window), 1)
+    coefs = coefs[:, :LANES].T[:share]
+    coefs_ref[...] = coefs
     f = forward_ref[...].astype(jnp.float32)
     b = backward_ref[...].astype(jnp.float32)
     rows = jnp.concatenate([f, b, f, b], axis=0).T
     state_ref[...] = rows
-    write_tile(rows, coefs_ref[...], tile_ref)
+    write_tile(rows, coefs, tile_ref)
 
 
 def pass_kernel(previous_ref, next_ref, coefs_ref, tile_ref, state_ref):
@@ -138,18 +181,19 @@
     backward_ref[...] = state[32:64].astype(jnp.bfloat16)
 
 
-def local(kernel, outs, scratch, flops, *args, scalars=0):
-    vmem = pl.BlockSpec(memory_space=pltpu.VMEM)
+def local(kernel, outs, scratch, flops, *args, scalars=0, space=pltpu.VMEM, vmem=16):
+    onchip = pl.BlockSpec(memory_space=pltpu.VMEM)
+    given = pl.BlockSpec(memory_space=space)
     smem = pl.BlockSpec(memory_space=pltpu.SMEM)
     moved = sum(a.size * a.dtype.itemsize for a in (*args, *outs))
     return pl.pallas_call(
         kernel,
         out_shape=outs,
-        in_specs=[smem] * scalars + [vmem] * (len(args) - scalars),
-        out_specs=tuple(vmem for _ in outs),
+        in_specs=[smem] * scalars + [given] * (len(args) - scalars),
+        out_specs=tuple(onchip for _ in outs),
         scratch_shapes=scratch,
         cost_estimate=pl.CostEstimate(flops=flops, bytes_accessed=moved, transcendentals=0),
-        compiler_params=pltpu.CompilerParams(vmem_limit_bytes=16 * 2**20),
+        compiler_params=pltpu.CompilerParams(vmem_limit_bytes=vmem * 2**20),
     )(*args)
 
 
@@ -164,23 +208,37 @@
     tile = (64, LANES)
     half = jnp.bfloat16
 
-    gain = lax.dynamic_slice_in_dim(norm_gain, me * share, share, 1)
-    router = lax.dynamic_slice_in_dim(router_weight[0], me * share, share, 1)
-    coefs = jnp.concatenate([gain, router * gain, jnp.zeros((3, share), jnp.float32)], axis=0).T
-    both = route_ids[:, :, 0].transpose(0, 3, 1, 2).reshape(steps_total, 2, -1)
-    both = jnp.concatenate([both, both], axis=2)
-
     entry_outs = (
         jax.ShapeDtypeStruct((sizes[1], *tile), half),
         jax.ShapeDtypeStruct((share, LANES), jnp.float32),
     )
-    copies, state = local(
-        enter_kernel, entry_outs, [], 0, forward_rows[0], backward_rows[0], coefs
-    )
-    in_t = w_gate_up[0].T
+    copies, state, coefs = local(
+        enter_kernel,
+        (*entry_outs, jax.ShapeDtypeStruct((share, 8), jnp.float32)),
+        [
+            pltpu.VMEM(forward_rows.shape[1:], half),
+            pltpu.VMEM(backward_rows.shape[1:], half),
+            pltpu.VMEM(norm_gain.shape, jnp.float32),
+            pltpu.VMEM(router_weight.shape[1:], jnp.float32),
+            pltpu.SemaphoreType.DMA((4,)),
+        ],
+        0,
+        me.reshape(1),
+        forward_rows[0],
+        backward_rows[0],
+        norm_gain,
+        router_weight[0],
+        scalars=1,
+        space=pltpu.HBM,
+        vmem=VMEM_MIB,
+    )
+    copies, packed_in, route_ids = lax.optimization_barrier((copies, w_gate_up, route_ids))
+    in_t = packed_in[0].T
+    both = route_ids[:, :, 0].transpose(0, 3, 1, 2).reshape(steps_total, 2, -1)
+    both = jnp.concatenate([both, both], axis=2)
     down_t = w_down[0].T
     for moment in range(steps_total):
-        rows = gathered(copies)
+        rows, (in_t, both) = gathered(copies, (in_t, both))
         (hidden,) = local(
             lambda *refs: hidden_kernel(sizes, width, *refs),
             (jax.ShapeDtypeStruct((sizes[1], 32, LANES), half),),
@@ -192,7 +250,7 @@
             both[moment],
             scalars=1,
         )
-        units = gathered(hidden)
+        units, _ = gathered(hidden)
         scratch = [pltpu.VMEM((all_units, LANES), half)]
         flops = 2 * all_units * share * LANES
         if moment + 1 < steps_total:

time: 210 us -> 218 us (1.038)
  the two profiles are of different devices: /device:TPU:2 before, /device:TPU:32 now
where the time goes in v3:
time: 218 us; the launch traced here: 217 us
  blocking collectives  106 us (49%)
  waiting for transfers between devices  55.8 us (26%)
  starting transfers between devices  43.7 us (20%)
  Pallas kernels  5.57 us (3%)
  local copies, waits for them, and re-layouts  5.55 us (3%)
    all_to_all x5, blocking collectives, everyone(): return lax.all_to_all(copies, axes, 0, 0)  106 us
    all_to_all x3, waiting for transfers between devices, everyone(): return lax.all_to_all(copies, axes, 0, 0)  54.4 us
    all_to_all x3, starting transfers between devices, everyone(): return lax.all_to_all(copies, axes, 0, 0)  38.1 us
    pallas_call x6, Pallas kernels, local(): pl.pallas_call(kernel, out_shape=outs, in_specs=[smem] * scalars + [given...  5.57 us
    ppermute x2, starting transfers between devices, passed_along(): return lax.ppermute(block, axis, route)  5.56 us
  transfers between devices with their start and end apart: 5, of which 4 were waited for; matrix products, arithmetic and copies ran while one was open for 1% of the time, Pallas kernels for 0%

profile of v3, /device:TPU:32, one launch (start us, length us, event | category | flops | bytes accessed | tf_op | source)
XLA Modules:
  0.0 217.4 jit_solution(4638495415722013839)
XLA Ops:
  0.6 2.0 shard_map.86
  2.6 27.4 %all-to-all-start = ((bf16[4,64,128]{2,1,0:T(8,128)(2,1)}), bf16[4,64,128]{2,1,0:T(8,128)(2,1)S(1)}, u32[]{:S(2)}, u32[]{:S(2)}) async-start(bf16[4,64,128]{2,1,0:T(8,128)(2,1)} %get-tuple-element.19), calls=%async_computation | async-start | bytes 131072 | tf_op jit(solution)/shard_map/all_to_all | solution.py:24
  30.1 0.0 copy-start.4
  30.1 2.8 %copy.9 = bf16[1,7168,128]{1,2,0:T(8,128)(2,1)S(1)} copy(bf16[1,7168,128]{2,1,0:T(8,128)(2,1)} %param.12) | data formatting | bytes 3670016 | tf_op jit(solution)/shard_map/optimization_barrier | solution.py:235
  32.9 0.0 copy-done.4
  32.9 0.1 reshape.31
  33.0 0.1 pad_add_fusion
  33.1 21.7 %all-to-all-done = bf16[4,64,128]{2,1,0:T(8,128)(2,1)S(1)} async-done(((bf16[4,64,128]{2,1,0:T(8,128)(2,1)}), bf16[4,64,128]{2,1,0:T(8,128)(2,1)S(1)}, u32[]{:S(2)}, u32[]{:S(2)}) %all-to-all-start) | async-done | bytes 65568 | tf_op jit(solution)/shard_map/all_to_all | solution.py:24
  54.8 1.2 broadcast_in_dim.12
  56.0 7.0 %all-to-all-start.1 = ((bf16[16,4,64,128]{3,2,1,0:T(8,128)(2,1)}), bf16[16,4,64,128]{3,2,1,0:T(8,128)(2,1)S(1)}, u32[]{:S(2)}, u32[]{:S(2)}) async-start(bf16[16,4,64,128]{3,2,1,0:T(8,128)(2,1)} %broadcast_in_dim.12), calls=%async_computation.1 | async-start | bytes 2097152 | tf_op jit(solution)/shard_map/all_to_all | solution.py:24
  63.1 14.4 %all-to-all-done.1 = bf16[16,4,64,128]{3,2,1,0:T(8,128)(2,1)S(1)} async-done(((bf16[16,4,64,128]{3,2,1,0:T(8,128)(2,1)}), bf16[16,4,64,128]{3,2,1,0:T(8,128)(2,1)S(1)}, u32[]{:S(2)}, u32[]{:S(2)}) %all-to-all-start.1) | async-done | bytes 1048608 | tf_op jit(solution)/shard_map/all_to_all | solution.py:24
  77.5 0.0 copy-start
  77.5 0.0 copy-start.3
  77.5 0.8 shard_map.87
  78.3 0.0 copy-start.2
  78.3 25.1 %all_to_all.40 = bf16[4,32,128]{2,1,0:T(8,128)(2,1)S(1)} all-to-all(bf16[4,32,128]{2,1,0:T(8,128)(2,1)S(1)} %shard_map.87), channel_id=1, replica_groups=mesh['pipe'=16,'y'=4,'zh'=4,'x'=4] {'zh'}, dimensions={0} | all-to-all | bytes 65536 | tf_op jit(solution)/shard_map/all_to_all | solution.py:24
  103.4 0.1 broadcast_in_dim.13
  103.5 12.9 %all_to_all.41 = bf16[16,4,32,128]{3,2,1,0:T(8,128)(2,1)S(1)} all-to-all(bf16[16,4,32,128]{3,2,1,0:T(8,128)(2,1)S(1)} %broadcast_in_dim.13), channel_id=1, replica_groups=mesh['pipe'=16,'y'=4,'zh'=4,'x'=4] {'y','x'}, dimensions={0} | all-to-all | bytes 1048576 | tf_op jit(solution)/shard_map/all_to_all | solution.py:24
  116.5 0.0 copy-done
  116.5 0.0 copy-done.3
  116.5 0.6 shard_map.88
  117.0 1.9 collective-permute-start
  118.9 3.6 %collective-permute-start.1 = (bf16[64,128]{1,0:T(8,128)(2,1)S(1)}, bf16[64,128]{1,0:T(8,128)(2,1)S(1)}, u32[]{:S(2)}, u32[]{:S(2)}) collective-permute-start(bf16[64,128]{1,0:T(8,128)(2,1)S(1)} %shard_map.88), channel_id=1, source_target_pairs={{64,0},{128,64},{192,128},{256,192},{320,256},{384,320},{448,384},... | collective-permute-start | bytes 49160 | tf_op jit(solution)/shard_map/ppermute | solution.py:20
  122.6 0.0 collective-permute-done.previous_ref
  122.6 1.4 collective-permute-done.1.next_ref
  124.0 0.0 copy-done.2
  124.0 0.2 shard_map.89
  124.3 29.7 %all_to_all.42 = bf16[4,64,128]{2,1,0:T(8,128)(2,1)S(1)} all-to-all(bf16[4,64,128]{2,1,0:T(8,128)(2,1)S(1)} %get-tuple-element.27), channel_id=1, replica_groups=mesh['pipe'=16,'y'=4,'zh'=4,'x'=4] {'zh'}, dimensions={0} | all-to-all | bytes 131072 | tf_op jit(solution)/shard_map/all_to_all | solution.py:24
  154.0 1.2 broadcast_in_dim.14
  155.2 3.7 %all-to-all-start.5 = ((bf16[16,4,64,128]{3,2,1,0:T(8,128)(2,1)}), bf16[16,4,64,128]{3,2,1,0:T(8,128)(2,1)S(1)}, u32[]{:S(2)}, u32[]{:S(2)}) async-start(bf16[16,4,64,128]{3,2,1,0:T(8,128)(2,1)} %broadcast_in_dim.14), calls=%async_computation.5 | async-start | bytes 2097152 | tf_op jit(solution)/shard_map/all_to_all | solution.py:24
  158.9 18.3 %all-to-all-done.5 = bf16[16,4,64,128]{3,2,1,0:T(8,128)(2,1)S(1)} async-done(((bf16[16,4,64,128]{3,2,1,0:T(8,128)(2,1)}), bf16[16,4,64,128]{3,2,1,0:T(8,128)(2,1)S(1)}, u32[]{:S(2)}, u32[]{:S(2)}) %all-to-all-start.5) | async-done | bytes 1048608 | tf_op jit(solution)/shard_map/all_to_all | solution.py:24
  177.2 0.0 copy-start.1
  177.2 0.8 shard_map.90
  178.0 24.6 %all_to_all.43 = bf16[4,32,128]{2,1,0:T(8,128)(2,1)S(1)} all-to-all(bf16[4,32,128]{2,1,0:T(8,128)(2,1)S(1)} %shard_map.90), channel_id=1, replica_groups=mesh['pipe'=16,'y'=4,'zh'=4,'x'=4] {'zh'}, dimensions={0} | all-to-all | bytes 65536 | tf_op jit(solution)/shard_map/all_to_all | solution.py:24
  202.6 0.1 broadcast_in_dim.15
  202.7 13.6 %all_to_all.44 = bf16[16,4,32,128]{3,2,1,0:T(8,128)(2,1)S(1)} all-to-all(bf16[16,4,32,128]{3,2,1,0:T(8,128)(2,1)S(1)} %broadcast_in_dim.15), channel_id=1, replica_groups=mesh['pipe'=16,'y'=4,'zh'=4,'x'=4] {'y','x'}, dimensions={0} | all-to-all | bytes 1048576 | tf_op jit(solution)/shard_map/all_to_all | solution.py:24
  216.3 0.0 copy-done.1
  216.3 1.1 shard_map.91
  (3 shorter events, 0.0 us)
Async XLA Ops:
  2.6 52.1 %all-to-all-start = ((bf16[4,64,128]{2,1,0:T(8,128)(2,1)}), bf16[4,64,128]{2,1,0:T(8,128)(2,1)S(1)}, u32[]{:S(2)}, u32[]{:S(2)}) async-start(bf16[4,64,128]{2,1,0:T(8,128)(2,1)} %get-tuple-element.19), calls=%async_computation | async-start | bytes 131072 | tf_op jit(solution)/shard_map/all_to_all | solution.py:24
  30.1 2.8 %copy-start.4 = (s32[2,2,1,32,2]{3,4,2,1,0:T(2,128)S(1)}, s32[2,2,1,32,2]{3,4,2,1,0:T(2,128)}, u32[]{:S(2)}) copy-start(s32[2,2,1,32,2]{3,4,2,1,0:T(2,128)} %param.9) | copy-start | bytes 3076
  56.0 21.5 %all-to-all-start.1 = ((bf16[16,4,64,128]{3,2,1,0:T(8,128)(2,1)}), bf16[16,4,64,128]{3,2,1,0:T(8,128)(2,1)S(1)}, u32[]{:S(2)}, u32[]{:S(2)}) async-start(bf16[16,4,64,128]{3,2,1,0:T(8,128)(2,1)} %broadcast_in_dim.12), calls=%async_computation.1 | async-start | bytes 2097152 | tf_op jit(solution)/shard_map/all_to_all | solution.py:24
  77.5 39.0 %copy-start = (bf16[1,4096,112]{1,2,0:T(8,128)(2,1)S(1)}, bf16[1,4096,112]{1,2,0:T(8,128)(2,1)}, u32[]{:S(2)}) copy-start(bf16[1,4096,112]{1,2,0:T(8,128)(2,1)} %param.13) | copy-start | bytes 2752516
  77.5 39.0 %copy-start.3 = (f32[112,128]{1,0:T(8,128)S(1)}, f32[112,128]{1,0:T(8,128)}, u32[]{:S(2)}) copy-start(f32[112,128]{1,0:T(8,128)} %get-tuple-element.25.refs_2_) | copy-start | bytes 172036
  78.3 45.7 %copy-start.2 = (f32[112,8]{1,0:T(8,128)S(1)}, f32[112,8]{1,0:T(8,128)}, u32[]{:S(2)}) copy-start(f32[112,8]{1,0:T(8,128)} %get-tuple-element.26.coefs_ref) | copy-start | bytes 10756
  117.0 5.6 %collective-permute-start = (bf16[64,128]{1,0:T(8,128)(2,1)S(1)}, bf16[64,128]{1,0:T(8,128)(2,1)S(1)}, u32[]{:S(2)}, u32[]{:S(2)}) collective-permute-start(bf16[64,128]{1,0:T(8,128)(2,1)S(1)} %shard_map.88), channel_id=1, source_target_pairs={{0,64},{64,128},{128,192},{192,256},{256,320},{320,384},{384,448},... | collective-permute-start | bytes 49160 | tf_op jit(solution)/shard_map/ppermute | solution.py:20
  118.9 5.1 %collective-permute-start.1 = (bf16[64,128]{1,0:T(8,128)(2,1)S(1)}, bf16[64,128]{1,0:T(8,128)(2,1)S(1)}, u32[]{:S(2)}, u32[]{:S(2)}) collective-permute-start(bf16[64,128]{1,0:T(8,128)(2,1)S(1)} %shard_map.88), channel_id=1, source_target_pairs={{64,0},{128,64},{192,128},{256,192},{320,256},{384,320},{448,384},... | collective-permute-start | bytes 49160 | tf_op jit(solution)/shard_map/ppermute | solution.py:20
  155.2 22.0 %all-to-all-start.5 = ((bf16[16,4,64,128]{3,2,1,0:T(8,128)(2,1)}), bf16[16,4,64,128]{3,2,1,0:T(8,128)(2,1)S(1)}, u32[]{:S(2)}, u32[]{:S(2)}) async-start(bf16[16,4,64,128]{3,2,1,0:T(8,128)(2,1)} %broadcast_in_dim.14), calls=%async_computation.5 | async-start | bytes 2097152 | tf_op jit(solution)/shard_map/all_to_all | solution.py:24
  177.2 39.1 %copy-start.1 = (bf16[1,4096,112]{1,2,0:T(8,128)(2,1)S(1)}, bf16[1,4096,112]{1,2,0:T(8,128)(2,1)}, u32[]{:S(2)}) copy-start(bf16[1,4096,112]{1,2,0:T(8,128)(2,1)} %param.13) | copy-start | bytes 2752516

commit v4 on v3

--- a/solution.py
+++ b/solution.py
@@ -11,7 +11,6 @@
 EXPERT = ("y", "zh", "x")
 LANES = 128
 STATS = 16
-VMEM_MIB = 60
 
 
 def passed_along(block, axis, distance):
@@ -24,12 +23,11 @@
     return lax.all_to_all(copies, axes, 0, 0)
 
 
-def gathered(copies, meanwhile=()):
+def gathered(copies):
     column = everyone(copies, "zh")
-    column, meanwhile = lax.optimization_barrier((column, meanwhile))
     size = lax.axis_size(PLANE)
     full = everyone(jnp.broadcast_to(column[None], (size, *column.shape)), PLANE)
-    return full.reshape(-1, *copies.shape[1:]), meanwhile
+    return full.reshape(-1, *copies.shape[1:])
 
 
 def lower_lanes(shape):
@@ -123,8 +121,11 @@
     write_tile(rows, coefs_ref[...], tile_ref)
 
 
-def hidden_kernel(sizes, width, own_ref, gathered_ref, weight_ref, ids_ref, out_ref, rows_ref):
-    share = weight_ref.shape[1] // gathered_ref.shape[0]
+def hidden_kernel(
+    sizes, moment, sharers, me_ref, gathered_ref, weight_ref, ids_ref, out_ref, rows_ref
+):
+    width = weight_ref.shape[0]
+    share = weight_ref.shape[0] // gathered_ref.shape[0]
     stats = jnp.zeros((STATS, LANES), jnp.float32)
     for place in range(gathered_ref.shape[0]):
         tile = gathered_ref[place].astype(jnp.float32)
@@ -134,19 +135,24 @@
         stats = stats + tile[48:]
     stats = turned(stats[:8] + stats[8:])
     inverse = lax.rsqrt(stats[0:1] / width + EPSILON)
-    projected = jnp.dot(
-        weight_ref[...], rows_ref[...], preferred_element_type=jnp.float32
+    projected = lax.dot_general(
+        weight_ref[...],
+        rows_ref[...],
+        (((0,), (0,)), ((), ())),
+        preferred_element_type=jnp.float32,
     ) * inverse
     scores = 1.0 / (1.0 + jnp.exp(-(stats[1:5] * inverse)))
+    own = lax.div(me_ref[0], sharers)
+    chosen = jnp.concatenate([ids_ref[moment, 0], ids_ref[moment, 1]] * 2, axis=1)
     total = jnp.zeros((1, LANES), jnp.float32)
     mine = jnp.zeros((1, LANES), jnp.float32)
-    for k in range(ids_ref.shape[0]):
-        ids = ids_ref[k : k + 1, :]
+    for k in range(chosen.shape[0]):
+        ids = chosen[k : k + 1]
         picked = jnp.zeros((1, LANES), jnp.float32)
         for e in range(4):
             picked = jnp.where(ids == e, scores[e : e + 1], picked)
         total = total + picked
-        mine = mine + jnp.where(ids == own_ref[0], picked, 0.0)
+        mine = mine + jnp.where(ids == own, picked, 0.0)
     weight = ROUTE_SCALE * (mine / total)
     gate, up = projected[:64], projected[64:]
     hidden = gate / (1.0 + jnp.exp(-gate)) * up * weight
@@ -202,8 +208,8 @@
     share = forward_rows.shape[2]
     width, columns = w_gate_up.shape[1:]
     all_units = w_down.shape[1]
-    me = lax.axis_index(EXPERT)
-    own = (me * (columns // 2) // (all_units // router_weight.shape[1])).reshape(1)
+    me = lax.axis_index(EXPERT).reshape(1)
+    sharers = all_units // router_weight.shape[1] // (columns // 2)
     steps_total = route_ids.shape[0]
     tile = (64, LANES)
     half = jnp.bfloat16
@@ -223,34 +229,31 @@
             pltpu.SemaphoreType.DMA((4,)),
         ],
         0,
-        me.reshape(1),
-        forward_rows[0],
-        backward_rows[0],
-        norm_gain,
-        router_weight[0],
+        me,
+        *(
+            pltpu.with_memory_space_constraint(a, pltpu.HBM)
+            for a in (forward_rows[0], backward_rows[0], norm_gain, router_weight[0])
+        ),
         scalars=1,
         space=pltpu.HBM,
-        vmem=VMEM_MIB,
-    )
-    copies, packed_in, route_ids = lax.optimization_barrier((copies, w_gate_up, route_ids))
-    in_t = packed_in[0].T
-    both = route_ids[:, :, 0].transpose(0, 3, 1, 2).reshape(steps_total, 2, -1)
-    both = jnp.concatenate([both, both], axis=2)
+    )
+    packed_in = w_gate_up[0]
+    chosen = route_ids[:, :, 0].transpose(0, 1, 3, 2)
     down_t = w_down[0].T
     for moment in range(steps_total):
-        rows, (in_t, both) = gathered(copies, (in_t, both))
+        rows = gathered(copies)
         (hidden,) = local(
-            lambda *refs: hidden_kernel(sizes, width, *refs),
+            lambda *refs: hidden_kernel(sizes, moment, sharers, *refs),
             (jax.ShapeDtypeStruct((sizes[1], 32, LANES), half),),
             [pltpu.VMEM((width, LANES), half)],
             2 * width * columns * LANES,
-            own,
+            me,
             rows,
-            in_t,
-            both[moment],
+            packed_in,
+            chosen,
             scalars=1,
         )
-        units, _ = gathered(hidden)
+        units = gathered(hidden)
         scratch = [pltpu.VMEM((all_units, LANES), half)]
         flops = 2 * all_units * share * LANES
         if moment + 1 < steps_total:

time: 218 us -> 207 us (0.950)
  the two profiles are of different devices: /device:TPU:32 before, /device:TPU:2 now
where the time goes in v4:
time: 207 us
  blocking collectives  194 us (94%)
  Pallas kernels  5.74 us (3%)
  starting transfers between devices  4.32 us (2%)
    all_to_all x8, blocking collectives, everyone(): return lax.all_to_all(copies, axes, 0, 0)  194 us
    pallas_call x6, Pallas kernels, local(): pl.pallas_call(kernel, out_shape=outs, in_specs=[smem] * scalars + [given...  5.74 us
    ppermute x2, starting transfers between devices, passed_along(): return lax.ppermute(block, axis, route)  4.32 us
  transfers between devices with their start and end apart: 2, of which 1 were waited for; matrix products, arithmetic and copies ran while one was open for 0% of the time, Pallas kernels for 0%

profile of v4, /device:TPU:2, one launch (start us, length us, event | category | flops | bytes accessed | tf_op | source)
XLA Modules:
  0.0 206.5 jit_solution(5992272412169711936)
XLA Ops:
  0.6 0.0 copy-start
  0.6 0.0 copy-start.2
  0.7 1.5 shard_map.86
  2.2 50.9 %all_to_all.40 = bf16[4,64,128]{2,1,0:T(8,128)(2,1)S(1)} all-to-all(bf16[4,64,128]{2,1,0:T(8,128)(2,1)S(1)} %get-tuple-element.9), channel_id=1, replica_groups=mesh['pipe'=16,'y'=4,'zh'=4,'x'=4] {'zh'}, dimensions={0} | all-to-all | bytes 131072 | tf_op jit(solution)/shard_map/all_to_all | solution.py:23
  53.1 0.2 broadcast_in_dim.12
  53.3 22.1 %all_to_all.41 = bf16[16,4,64,128]{3,2,1,0:T(8,128)(2,1)S(1)} all-to-all(bf16[16,4,64,128]{3,2,1,0:T(8,128)(2,1)S(1)} %broadcast_in_dim.12), channel_id=1, replica_groups=mesh['pipe'=16,'y'=4,'zh'=4,'x'=4] {'y','x'}, dimensions={0} | all-to-all | bytes 2097152 | tf_op jit(solution)/shard_map/all_to_all | solution.py:23
  75.4 0.0 copy-done
  75.4 0.0 copy-done.2
  75.5 0.0 copy-start.1
  75.5 1.1 shard_map.87
  76.6 24.6 %all_to_all.42 = bf16[4,32,128]{2,1,0:T(8,128)(2,1)S(1)} all-to-all(bf16[4,32,128]{2,1,0:T(8,128)(2,1)S(1)} %shard_map.87), channel_id=1, replica_groups=mesh['pipe'=16,'y'=4,'zh'=4,'x'=4] {'zh'}, dimensions={0} | all-to-all | bytes 65536 | tf_op jit(solution)/shard_map/all_to_all | solution.py:23
  101.2 0.1 broadcast_in_dim.13
  101.3 13.1 %all_to_all.43 = bf16[16,4,32,128]{3,2,1,0:T(8,128)(2,1)S(1)} all-to-all(bf16[16,4,32,128]{3,2,1,0:T(8,128)(2,1)S(1)} %broadcast_in_dim.13), channel_id=1, replica_groups=mesh['pipe'=16,'y'=4,'zh'=4,'x'=4] {'y','x'}, dimensions={0} | all-to-all | bytes 1048576 | tf_op jit(solution)/shard_map/all_to_all | solution.py:23
  114.4 0.0 copy-done.1
  114.4 0.6 shard_map.88
  115.0 1.3 collective-permute-start.1
  116.3 3.0 %collective-permute-start = (bf16[64,128]{1,0:T(8,128)(2,1)S(1)}, bf16[64,128]{1,0:T(8,128)(2,1)S(1)}, u32[]{:S(2)}, u32[]{:S(2)}) collective-permute-start(bf16[64,128]{1,0:T(8,128)(2,1)S(1)} %shard_map.88), channel_id=1, source_target_pairs={{0,64},{64,128},{128,192},{192,256},{256,320},{320,384},{384,448},... | collective-permute-start | bytes 49160 | tf_op jit(solution)/shard_map/ppermute | solution.py:19
  119.3 0.0 collective-permute-done.1.next_ref
  119.3 0.8 collective-permute-done.previous_ref
  120.1 0.2 shard_map.89
  120.4 25.9 %all_to_all.44 = bf16[4,64,128]{2,1,0:T(8,128)(2,1)S(1)} all-to-all(bf16[4,64,128]{2,1,0:T(8,128)(2,1)S(1)} %get-tuple-element.12), channel_id=1, replica_groups=mesh['pipe'=16,'y'=4,'zh'=4,'x'=4] {'zh'}, dimensions={0} | all-to-all | bytes 131072 | tf_op jit(solution)/shard_map/all_to_all | solution.py:23
  146.3 0.2 broadcast_in_dim.14
  146.5 19.2 %all_to_all.45 = bf16[16,4,64,128]{3,2,1,0:T(8,128)(2,1)S(1)} all-to-all(bf16[16,4,64,128]{3,2,1,0:T(8,128)(2,1)S(1)} %broadcast_in_dim.14), channel_id=1, replica_groups=mesh['pipe'=16,'y'=4,'zh'=4,'x'=4] {'y','x'}, dimensions={0} | all-to-all | bytes 2097152 | tf_op jit(solution)/shard_map/all_to_all | solution.py:23
  165.7 1.1 shard_map.90
  166.8 25.4 %all_to_all.46 = bf16[4,32,128]{2,1,0:T(8,128)(2,1)S(1)} all-to-all(bf16[4,32,128]{2,1,0:T(8,128)(2,1)S(1)} %shard_map.90), channel_id=1, replica_groups=mesh['pipe'=16,'y'=4,'zh'=4,'x'=4] {'zh'}, dimensions={0} | all-to-all | bytes 65536 | tf_op jit(solution)/shard_map/all_to_all | solution.py:23
  192.2 0.1 broadcast_in_dim.15
  192.3 13.1 %all_to_all.47 = bf16[16,4,32,128]{3,2,1,0:T(8,128)(2,1)S(1)} all-to-all(bf16[16,4,32,128]{3,2,1,0:T(8,128)(2,1)S(1)} %broadcast_in_dim.15), channel_id=1, replica_groups=mesh['pipe'=16,'y'=4,'zh'=4,'x'=4] {'y','x'}, dimensions={0} | all-to-all | bytes 1048576 | tf_op jit(solution)/shard_map/all_to_all | solution.py:23
  205.4 1.1 shard_map.91
Async XLA Ops:
  0.6 74.8 %copy-start = (bf16[1,7168,128]{2,1,0:T(8,128)(2,1)S(1)}, bf16[1,7168,128]{2,1,0:T(8,128)(2,1)}, u32[]{:S(2)}) copy-start(bf16[1,7168,128]{2,1,0:T(8,128)(2,1)} %param.12) | copy-start | bytes 5505028
  0.6 74.8 %copy-start.2 = (s32[2,2,1,32,2]{3,4,2,1,0:T(2,128)S(1)}, s32[2,2,1,32,2]{3,4,2,1,0:T(2,128)}, u32[]{:S(2)}) copy-start(s32[2,2,1,32,2]{3,4,2,1,0:T(2,128)} %param.9) | copy-start | bytes 3076
  75.5 39.0 %copy-start.1 = (bf16[1,4096,112]{1,2,0:T(8,128)(2,1)S(1)}, bf16[1,4096,112]{1,2,0:T(8,128)(2,1)}, u32[]{:S(2)}) copy-start(bf16[1,4096,112]{1,2,0:T(8,128)(2,1)} %param.13) | copy-start | bytes 2752516
  115.0 4.3 %collective-permute-start.1 = (bf16[64,128]{1,0:T(8,128)(2,1)S(1)}, bf16[64,128]{1,0:T(8,128)(2,1)S(1)}, u32[]{:S(2)}, u32[]{:S(2)}) collective-permute-start(bf16[64,128]{1,0:T(8,128)(2,1)S(1)} %shard_map.88), channel_id=1, source_target_pairs={{64,0},{128,64},{192,128},{256,192},{320,256},{384,320},{448,384},... | collective-permute-start | bytes 49160 | tf_op jit(solution)/shard_map/ppermute | solution.py:19
  116.3 3.9 %collective-permute-start = (bf16[64,128]{1,0:T(8,128)(2,1)S(1)}, bf16[64,128]{1,0:T(8,128)(2,1)S(1)}, u32[]{:S(2)}, u32[]{:S(2)}) collective-permute-start(bf16[64,128]{1,0:T(8,128)(2,1)S(1)} %shard_map.88), channel_id=1, source_target_pairs={{0,64},{64,128},{128,192},{192,256},{256,320},{320,384},{384,448},... | collective-permute-start | bytes 49160 | tf_op jit(solution)/shard_map/ppermute | solution.py:19

commit v5 on v4

--- a/solution.py
+++ b/solution.py
@@ -8,6 +8,7 @@
 EPSILON = 1e-06
 ROUTE_SCALE = 2.5
 PLANE = ("y", "x")
+ROW = ("zh", "x")
 EXPERT = ("y", "zh", "x")
 LANES = 128
 STATS = 16
@@ -23,10 +24,19 @@
     return lax.all_to_all(copies, axes, 0, 0)
 
 
-def gathered(copies):
-    column = everyone(copies, "zh")
-    size = lax.axis_size(PLANE)
-    full = everyone(jnp.broadcast_to(column[None], (size, *column.shape)), PLANE)
+def spread(block, axes):
+    size = lax.axis_size(axes)
+    return everyone(jnp.broadcast_to(block[None], (size, *block.shape)), axes)
+
+
+def gathered_rows(copies, by_gather):
+    row = everyone(copies, ROW)
+    full = lax.all_gather(row, "y") if by_gather else spread(row, "y")
+    return full.reshape(-1, *copies.shape[1:])
+
+
+def gathered_units(copies):
+    full = spread(everyone(copies, "zh"), PLANE)
     return full.reshape(-1, *copies.shape[1:])
 
 
@@ -122,14 +132,14 @@
 
 
 def hidden_kernel(
-    sizes, moment, sharers, me_ref, gathered_ref, weight_ref, ids_ref, out_ref, rows_ref
+    moment, sharers, me_ref, gathered_ref, weight_ref, ids_ref, out_ref, rows_ref
 ):
     width = weight_ref.shape[0]
     share = weight_ref.shape[0] // gathered_ref.shape[0]
     stats = jnp.zeros((STATS, LANES), jnp.float32)
     for place in range(gathered_ref.shape[0]):
         tile = gathered_ref[place].astype(jnp.float32)
-        start = natural(place, sizes) * share
+        start = place * share
         rows_ref[start : start + 64, :] = gathered_ref[place]
         rows_ref[start + 64 : start + share, :] = turned(tile[:48]).astype(jnp.bfloat16)
         stats = stats + tile[48:]
@@ -215,7 +225,7 @@
     half = jnp.bfloat16
 
     entry_outs = (
-        jax.ShapeDtypeStruct((sizes[1], *tile), half),
+        jax.ShapeDtypeStruct((sizes[1] * sizes[2], *tile), half),
         jax.ShapeDtypeStruct((share, LANES), jnp.float32),
     )
     copies, state, coefs = local(
@@ -241,9 +251,9 @@
     chosen = route_ids[:, :, 0].transpose(0, 1, 3, 2)
     down_t = w_down[0].T
     for moment in range(steps_total):
-        rows = gathered(copies)
+        rows = gathered_rows(copies, moment == 0)
         (hidden,) = local(
-            lambda *refs: hidden_kernel(sizes, moment, sharers, *refs),
+            lambda *refs: hidden_kernel(moment, sharers, *refs),
             (jax.ShapeDtypeStruct((sizes[1], 32, LANES), half),),
             [pltpu.VMEM((width, LANES), half)],
             2 * width * columns * LANES,
@@ -253,7 +263,7 @@
             chosen,
             scalars=1,
         )
-        units = gathered(hidden)
+        units = gathered_units(hidden)
         scratch = [pltpu.VMEM((all_units, LANES), half)]
         flops = 2 * all_units * share * LANES
         if moment + 1 < steps_total:

time: 207 us -> 292 us (1.41)
  waiting for transfers between devices: 0.81 us -> 36.4 us
  blocking collectives: 194 us -> 227 us
  between operations: 0.73 us -> 14.1 us
  local copies, waits for them, and re-layouts: 0.68 us -> 3.85 us
    all_gather x0 -> x1, waiting for transfers between devices: none -> 35.5 us  [gathered_rows(): full = lax.all_gather(row, 'y') if by_gather else spread(row, 'y')]
    all_to_all x8 -> x7, blocking collectives: 194 us -> 227 us  [everyone(): return lax.all_to_all(copies, axes, 0, 0)]
    unnamed x6 -> x12, local copies, waits for them, and re-layouts: 0.01 us -> 3.42 us
  transfers between devices with their start and end apart: 2 -> 3, of which waited for: 1 -> 2; matrix products, arithmetic and copies ran while one was open for 0% -> 0% of each run, Pallas kernels for 0% -> 0%
where the time goes in v5:
time: 292 us; the launch traced here: 291 us
  blocking collectives  227 us (78%)
  waiting for transfers between devices  36.4 us (12%)
  between operations  14.1 us (5%)
  Pallas kernels  5.55 us (2%)
  starting transfers between devices  4.35 us (1%)
  local copies, waits for them, and re-layouts  3.85 us (1%)
    all_to_all x7, blocking collectives, everyone(): return lax.all_to_all(copies, axes, 0, 0)  227 us
    all_gather x1, waiting for transfers between devices, gathered_rows(): full = lax.all_gather(row, 'y') if by_gather else spread(row, 'y')  35.5 us
  transfers between devices with their start and end apart: 3, of which 2 were waited for; matrix products, arithmetic and copies ran while one was open for 0% of the time, Pallas kernels for 0%

profile of v5, /device:TPU:2, one launch (start us, length us, event | category | flops | bytes accessed | tf_op | source)
XLA Modules:
  0.0 290.9 jit_solution(11971311726755632925)
XLA Ops:
  7.2 0.0 all-gather.3.cloned.1.call-start
  7.2 1.4 shard_map.86
  8.6 64.0 %all_to_all.35 = bf16[16,64,128]{2,1,0:T(8,128)(2,1)} all-to-all(bf16[16,64,128]{2,1,0:T(8,128)(2,1)S(1)} %get-tuple-element.9), channel_id=1, replica_groups=mesh['pipe'=16,'y'=4,'zh'=4,'x'=4] {'zh','x'}, dimensions={0} | all-to-all | bytes 524288 | tf_op jit(solution)/shard_map/all_to_all | solution.py:24
  72.6 0.0 all-gather.3.cloned.1.call-update
  72.6 35.5 %all-gather.3.cloned.1.call-done.refs_1_ = bf16[64,64,128]{2,1,0:T(8,128)(2,1)} async-done(((bf16[16,64,128]{2,1,0:T(8,128)(2,1)}), bf16[64,64,128]{2,1,0:T(8,128)(2,1)}) %all-gather.3.cloned.1.call-update) | async-done | bytes 1048592 | tf_op jit(solution)/shard_map/all_gather | solution.py:34
  108.1 0.0 copy-start
  108.1 1.5 copy-done
  109.6 0.0 copy-start.3
  109.6 1.2 copy-done.3
  110.9 0.0 copy-start.4
  110.9 0.7 copy-done.4
  111.6 0.0 copy-start.2
  111.6 1.1 shard_map.87
  112.7 44.6 %all_to_all.36 = bf16[4,32,128]{2,1,0:T(8,128)(2,1)S(1)} all-to-all(bf16[4,32,128]{2,1,0:T(8,128)(2,1)S(1)} %shard_map.87), channel_id=1, replica_groups=mesh['pipe'=16,'y'=4,'zh'=4,'x'=4] {'zh'}, dimensions={0} | all-to-all | bytes 65536 | tf_op jit(solution)/shard_map/all_to_all | solution.py:24
  157.3 0.1 broadcast_in_dim.10
  157.4 14.9 %all_to_all.37 = bf16[16,4,32,128]{3,2,1,0:T(8,128)(2,1)S(1)} all-to-all(bf16[16,4,32,128]{3,2,1,0:T(8,128)(2,1)S(1)} %broadcast_in_dim.10), channel_id=1, replica_groups=mesh['pipe'=16,'y'=4,'zh'=4,'x'=4] {'y','x'}, dimensions={0} | all-to-all | bytes 1048576 | tf_op jit(solution)/shard_map/all_to_all | solution.py:24
  172.2 0.0 copy-done.2
  172.2 0.6 shard_map.88
  172.8 1.3 collective-permute-start.1
  174.1 3.0 %collective-permute-start = (bf16[64,128]{1,0:T(8,128)(2,1)S(1)}, bf16[64,128]{1,0:T(8,128)(2,1)S(1)}, u32[]{:S(2)}, u32[]{:S(2)}) collective-permute-start(bf16[64,128]{1,0:T(8,128)(2,1)S(1)} %shard_map.88), channel_id=1, source_target_pairs={{0,64},{64,128},{128,192},{192,256},{256,320},{320,384},{384,448},... | collective-permute-start | bytes 49160 | tf_op jit(solution)/shard_map/ppermute | solution.py:20
  177.1 0.0 collective-permute-done.1.next_ref
  177.1 0.8 collective-permute-done.previous_ref
  178.0 0.3 shard_map.89
  178.2 36.1 %all_to_all.38 = bf16[16,64,128]{2,1,0:T(8,128)(2,1)S(1)} all-to-all(bf16[16,64,128]{2,1,0:T(8,128)(2,1)S(1)} %get-tuple-element.12), channel_id=1, replica_groups=mesh['pipe'=16,'y'=4,'zh'=4,'x'=4] {'zh','x'}, dimensions={0} | all-to-all | bytes 524288 | tf_op jit(solution)/shard_map/all_to_all | solution.py:24
  214.3 0.0 copy-start.1
  214.3 0.0 copy-start.5
  214.4 0.2 broadcast_in_dim.11
  214.6 17.8 %all_to_all.39 = bf16[4,16,64,128]{3,2,1,0:T(8,128)(2,1)S(1)} all-to-all(bf16[4,16,64,128]{3,2,1,0:T(8,128)(2,1)S(1)} %broadcast_in_dim.11), channel_id=1, replica_groups=mesh['pipe'=16,'y'=4,'zh'=4,'x'=4] {'y'}, dimensions={0} | all-to-all | bytes 2097152 | tf_op jit(solution)/shard_map/all_to_all | solution.py:24
  232.4 0.0 copy-done.1
  232.5 0.0 copy-done.5
  232.5 1.1 shard_map.90
  233.6 35.0 %all_to_all.40 = bf16[4,32,128]{2,1,0:T(8,128)(2,1)S(1)} all-to-all(bf16[4,32,128]{2,1,0:T(8,128)(2,1)S(1)} %shard_map.90), channel_id=1, replica_groups=mesh['pipe'=16,'y'=4,'zh'=4,'x'=4] {'zh'}, dimensions={0} | all-to-all | bytes 65536 | tf_op jit(solution)/shard_map/all_to_all | solution.py:24
  268.5 0.1 broadcast_in_dim.12
  268.6 14.2 %all_to_all.41 = bf16[16,4,32,128]{3,2,1,0:T(8,128)(2,1)S(1)} all-to-all(bf16[16,4,32,128]{3,2,1,0:T(8,128)(2,1)S(1)} %broadcast_in_dim.12), channel_id=1, replica_groups=mesh['pipe'=16,'y'=4,'zh'=4,'x'=4] {'y','x'}, dimensions={0} | all-to-all | bytes 1048576 | tf_op jit(solution)/shard_map/all_to_all | solution.py:24
  282.9 1.1 shard_map.91
Async XLA Ops:
  7.2 101.0 %all-gather.3.cloned.1.call-start = ((), (), s32[]{:S(2)}) async-start(), calls=%async_computation.7 | async-start | bytes 1310720 | tf_op jit(solution)/shard_map/all_gather | solution.py:34
  108.1 1.5 copy-start
  109.6 1.2 copy-start.3
  110.9 0.7 copy-start.4
  111.6 60.7 %copy-start.2 = (bf16[1,4096,112]{1,2,0:T(8,128)(2,1)S(1)}, bf16[1,4096,112]{1,2,0:T(8,128)(2,1)}, u32[]{:S(2)}) copy-start(bf16[1,4096,112]{1,2,0:T(8,128)(2,1)} %param.13) | copy-start | bytes 2752516
  172.8 4.3 %collective-permute-start.1 = (bf16[64,128]{1,0:T(8,128)(2,1)S(1)}, bf16[64,128]{1,0:T(8,128)(2,1)S(1)}, u32[]{:S(2)}, u32[]{:S(2)}) collective-permute-start(bf16[64,128]{1,0:T(8,128)(2,1)S(1)} %shard_map.88), channel_id=1, source_target_pairs={{64,0},{128,64},{192,128},{256,192},{320,256},{384,320},{448,384},... | collective-permute-start | bytes 49160 | tf_op jit(solution)/shard_map/ppermute | solution.py:20
  174.1 3.9 %collective-permute-start = (bf16[64,128]{1,0:T(8,128)(2,1)S(1)}, bf16[64,128]{1,0:T(8,128)(2,1)S(1)}, u32[]{:S(2)}, u32[]{:S(2)}) collective-permute-start(bf16[64,128]{1,0:T(8,128)(2,1)S(1)} %shard_map.88), channel_id=1, source_target_pairs={{0,64},{64,128},{128,192},{192,256},{256,320},{320,384},{384,448},... | collective-permute-start | bytes 49160 | tf_op jit(solution)/shard_map/ppermute | solution.py:20
  214.3 18.1 %copy-start.1 = (bf16[1,7168,128]{2,1,0:T(8,128)(2,1)S(1)}, bf16[1,7168,128]{2,1,0:T(8,128)(2,1)}, u32[]{:S(2)}) copy-start(bf16[1,7168,128]{2,1,0:T(8,128)(2,1)} %param.12) | copy-start | bytes 5505028
  214.3 18.1 %copy-start.5 = (s32[2,2,1,32,2]{3,4,2,1,0:T(2,128)S(1)}, s32[2,2,1,32,2]{3,4,2,1,0:T(2,128)}, u32[]{:S(2)}) copy-start(s32[2,2,1,32,2]{3,4,2,1,0:T(2,128)} %param.9) | copy-start | bytes 3076
Sparse Core Ops, SparseCore 0:
  72.7 35.3 all-gather.2

commit v6 on v4

--- a/solution.py
+++ b/solution.py
@@ -19,15 +19,10 @@
     return lax.ppermute(block, axis, route)
 
 
-def everyone(copies, axes):
-    return lax.all_to_all(copies, axes, 0, 0)
-
-
-def gathered(copies):
-    column = everyone(copies, "zh")
-    size = lax.axis_size(PLANE)
-    full = everyone(jnp.broadcast_to(column[None], (size, *column.shape)), PLANE)
-    return full.reshape(-1, *copies.shape[1:])
+def gathered(tile):
+    column = lax.all_gather(tile, "zh")
+    copies = jnp.broadcast_to(column[None], (lax.axis_size(PLANE), *column.shape))
+    return lax.all_to_all(copies, PLANE, 0, 0).reshape(-1, *tile.shape)
 
 
 def lower_lanes(shape):
@@ -56,8 +51,7 @@
     upper = jnp.concatenate([scaled[64:], high, sums - high], axis=0)
     tile = jnp.where(lower_lanes((64, LANES)), scaled[:64], turned(upper))
     tile = tile.astype(jnp.bfloat16)
-    for copy in range(tile_ref.shape[0]):
-        tile_ref[copy] = tile
+    tile_ref[...] = tile
 
 
 def enter_kernel(
@@ -158,8 +152,7 @@
     hidden = gate / (1.0 + jnp.exp(-gate)) * up * weight
     folded = jnp.where(lower_lanes((32, LANES)), hidden[:32], turned(hidden[32:]))
     folded = folded.astype(jnp.bfloat16)
-    for copy in range(out_ref.shape[0]):
-        out_ref[copy] = folded
+    out_ref[...] = folded
 
 
 def updated(sizes, gathered_ref, weight_ref, state_ref, rows_ref):
@@ -215,10 +208,10 @@
     half = jnp.bfloat16
 
     entry_outs = (
-        jax.ShapeDtypeStruct((sizes[1], *tile), half),
+        jax.ShapeDtypeStruct(tile, half),
         jax.ShapeDtypeStruct((share, LANES), jnp.float32),
     )
-    copies, state, coefs = local(
+    sent, state, coefs = local(
         enter_kernel,
         (*entry_outs, jax.ShapeDtypeStruct((share, 8), jnp.float32)),
         [
@@ -241,10 +234,10 @@
     chosen = route_ids[:, :, 0].transpose(0, 1, 3, 2)
     down_t = w_down[0].T
     for moment in range(steps_total):
-        rows = gathered(copies)
+        rows = gathered(sent)
         (hidden,) = local(
             lambda *refs: hidden_kernel(sizes, moment, sharers, *refs),
-            (jax.ShapeDtypeStruct((sizes[1], 32, LANES), half),),
+            (jax.ShapeDtypeStruct((32, LANES), half),),
             [pltpu.VMEM((width, LANES), half)],
             2 * width * columns * LANES,
             me,
@@ -266,7 +259,7 @@
                 down_t,
                 state,
             )
-            copies, state = local(
+            sent, state = local(
                 pass_kernel,
                 entry_outs,
                 [],

time: 207 us -> 202 us (0.976)
  blocking collectives: 194 us -> 189 us
    all_to_all x8 -> x4, blocking collectives: 194 us -> 64.4 us  [gathered(): return lax.all_to_all(copies, PLANE, 0, 0).reshape(-1, *tile.shape)]
    all_gather x0 -> x4, blocking collectives: none -> 125 us  [gathered(): column = lax.all_gather(tile, 'zh')]
where the time goes in v6:
time: 202 us; the launch traced here: 201 us
  blocking collectives  189 us (94%)
  Pallas kernels  5.73 us (3%)
  starting transfers between devices  4.32 us (2%)
    all_gather x4, blocking collectives, gathered(): column = lax.all_gather(tile, 'zh')  125 us
    all_to_all x4, blocking collectives, gathered(): return lax.all_to_all(copies, PLANE, 0, 0).reshape(-1, *tile.shape)  64.4 us
    pallas_call x6, Pallas kernels, local(): pl.pallas_call(kernel, out_shape=outs, in_specs=[smem] * scalars + [given...  5.73 us
    ppermute x2, starting transfers between devices, passed_along(): return lax.ppermute(block, axis, route)  4.32 us
  transfers between devices with their start and end apart: 2, of which 1 were waited for; matrix products, arithmetic and copies ran while one was open for 0% of the time, Pallas kernels for 0%

profile of v6, /device:TPU:2, one launch (start us, length us, event | category | flops | bytes accessed | tf_op | source)
XLA Modules:
  0.0 201.3 jit_solution(10601094577312837075)
XLA Ops:
  0.6 0.0 copy-start
  0.6 0.0 copy-start.2
  0.7 1.5 shard_map.86
  2.2 43.8 %all-gather = bf16[256,128]{1,0:T(8,128)(2,1)S(1)} all-gather(bf16[64,128]{1,0:T(8,128)(2,1)S(1)} %get-tuple-element.9), channel_id=2, replica_groups=mesh['pipe'=16,'y'=4,'zh'=4,'x'=4] {'zh'}, dimensions={0}, use_global_device_ids=true | all-gather | bytes 81920 | tf_op jit(solution)/shard_map/all_gather | solution.py:23
  46.0 0.2 broadcast_in_dim.12
  46.3 20.2 %all_to_all.20 = bf16[16,4,64,128]{3,2,1,0:T(8,128)(2,1)S(1)} all-to-all(bf16[16,4,64,128]{3,2,1,0:T(8,128)(2,1)S(1)} %broadcast_in_dim.12), channel_id=1, replica_groups=mesh['pipe'=16,'y'=4,'zh'=4,'x'=4] {'y','x'}, dimensions={0} | all-to-all | bytes 2097152 | tf_op jit(solution)/shard_map/all_to_all | solution.py:25
  66.4 0.0 copy-done
  66.4 0.0 copy-done.2
  66.4 0.0 copy-start.1
  66.5 1.1 shard_map.87
  67.6 26.9 %all-gather.1 = bf16[128,128]{1,0:T(8,128)(2,1)S(1)} all-gather(bf16[32,128]{1,0:T(8,128)(2,1)S(1)} %shard_map.87), channel_id=3, replica_groups=mesh['pipe'=16,'y'=4,'zh'=4,'x'=4] {'zh'}, dimensions={0}, use_global_device_ids=true | all-gather | bytes 40960 | tf_op jit(solution)/shard_map/all_gather | solution.py:23
  94.5 0.1 broadcast_in_dim.13
  94.6 13.0 %all_to_all.21 = bf16[16,4,32,128]{3,2,1,0:T(8,128)(2,1)S(1)} all-to-all(bf16[16,4,32,128]{3,2,1,0:T(8,128)(2,1)S(1)} %broadcast_in_dim.13), channel_id=1, replica_groups=mesh['pipe'=16,'y'=4,'zh'=4,'x'=4] {'y','x'}, dimensions={0} | all-to-all | bytes 1048576 | tf_op jit(solution)/shard_map/all_to_all | solution.py:25
  107.6 0.0 copy-done.1
  107.6 0.6 shard_map.88
  108.2 1.3 collective-permute-start.1
  109.5 3.0 %collective-permute-start = (bf16[64,128]{1,0:T(8,128)(2,1)S(1)}, bf16[64,128]{1,0:T(8,128)(2,1)S(1)}, u32[]{:S(2)}, u32[]{:S(2)}) collective-permute-start(bf16[64,128]{1,0:T(8,128)(2,1)S(1)} %shard_map.88), channel_id=1, source_target_pairs={{0,64},{64,128},{128,192},{192,256},{256,320},{320,384},{384,448},... | collective-permute-start | bytes 49160 | tf_op jit(solution)/shard_map/ppermute | solution.py:19
  112.5 0.0 collective-permute-done.1.next_ref
  112.5 0.8 collective-permute-done.previous_ref
  113.3 0.2 shard_map.89
  113.6 26.9 %all-gather.2 = bf16[256,128]{1,0:T(8,128)(2,1)S(1)} all-gather(bf16[64,128]{1,0:T(8,128)(2,1)S(1)} %get-tuple-element.12), channel_id=4, replica_groups=mesh['pipe'=16,'y'=4,'zh'=4,'x'=4] {'zh'}, dimensions={0}, use_global_device_ids=true | all-gather | bytes 81920 | tf_op jit(solution)/shard_map/all_gather | solution.py:23
  140.5 0.2 broadcast_in_dim.14
  140.8 18.3 %all_to_all.22 = bf16[16,4,64,128]{3,2,1,0:T(8,128)(2,1)S(1)} all-to-all(bf16[16,4,64,128]{3,2,1,0:T(8,128)(2,1)S(1)} %broadcast_in_dim.14), channel_id=1, replica_groups=mesh['pipe'=16,'y'=4,'zh'=4,'x'=4] {'y','x'}, dimensions={0} | all-to-all | bytes 2097152 | tf_op jit(solution)/shard_map/all_to_all | solution.py:25
  159.0 1.1 shard_map.90
  160.2 26.9 %all-gather.3 = bf16[128,128]{1,0:T(8,128)(2,1)S(1)} all-gather(bf16[32,128]{1,0:T(8,128)(2,1)S(1)} %shard_map.90), channel_id=5, replica_groups=mesh['pipe'=16,'y'=4,'zh'=4,'x'=4] {'zh'}, dimensions={0}, use_global_device_ids=true | all-gather | bytes 40960 | tf_op jit(solution)/shard_map/all_gather | solution.py:23
  187.1 0.1 broadcast_in_dim.15
  187.2 13.0 %all_to_all.23 = bf16[16,4,32,128]{3,2,1,0:T(8,128)(2,1)S(1)} all-to-all(bf16[16,4,32,128]{3,2,1,0:T(8,128)(2,1)S(1)} %broadcast_in_dim.15), channel_id=1, replica_groups=mesh['pipe'=16,'y'=4,'zh'=4,'x'=4] {'y','x'}, dimensions={0} | all-to-all | bytes 1048576 | tf_op jit(solution)/shard_map/all_to_all | solution.py:25
  200.2 1.1 shard_map.91
Async XLA Ops:
  0.6 65.8 %copy-start = (bf16[1,7168,128]{2,1,0:T(8,128)(2,1)S(1)}, bf16[1,7168,128]{2,1,0:T(8,128)(2,1)}, u32[]{:S(2)}) copy-start(bf16[1,7168,128]{2,1,0:T(8,128)(2,1)} %param.12) | copy-start | bytes 5505028
  0.6 65.8 %copy-start.2 = (s32[2,2,1,32,2]{3,4,2,1,0:T(2,128)S(1)}, s32[2,2,1,32,2]{3,4,2,1,0:T(2,128)}, u32[]{:S(2)}) copy-start(s32[2,2,1,32,2]{3,4,2,1,0:T(2,128)} %param.9) | copy-start | bytes 3076
  66.4 41.2 %copy-start.1 = (bf16[1,4096,112]{1,2,0:T(8,128)(2,1)S(1)}, bf16[1,4096,112]{1,2,0:T(8,128)(2,1)}, u32[]{:S(2)}) copy-start(bf16[1,4096,112]{1,2,0:T(8,128)(2,1)} %param.13) | copy-start | bytes 2752516
  108.2 4.3 %collective-permute-start.1 = (bf16[64,128]{1,0:T(8,128)(2,1)S(1)}, bf16[64,128]{1,0:T(8,128)(2,1)S(1)}, u32[]{:S(2)}, u32[]{:S(2)}) collective-permute-start(bf16[64,128]{1,0:T(8,128)(2,1)S(1)} %shard_map.88), channel_id=1, source_target_pairs={{64,0},{128,64},{192,128},{256,192},{320,256},{384,320},{448,384},... | collective-permute-start | bytes 49160 | tf_op jit(solution)/shard_map/ppermute | solution.py:19
  109.5 3.9 %collective-permute-start = (bf16[64,128]{1,0:T(8,128)(2,1)S(1)}, bf16[64,128]{1,0:T(8,128)(2,1)S(1)}, u32[]{:S(2)}, u32[]{:S(2)}) collective-permute-start(bf16[64,128]{1,0:T(8,128)(2,1)S(1)} %shard_map.88), channel_id=1, source_target_pairs={{0,64},{64,128},{128,192},{192,256},{256,320},{320,384},{384,448},... | collective-permute-start | bytes 49160 | tf_op jit(solution)/shard_map/ppermute | solution.py:19

commit v7 on v6

--- a/solution.py
+++ b/solution.py
@@ -31,6 +31,11 @@
 
 def turned(value):
     return pltpu.roll(value, LANES // 2, 1)
+
+
+def exchanged(value):
+    half = LANES // 2
+    return jnp.concatenate([value[:, half:], value[:, :half]], axis=1)
 
 
 def natural(place, sizes):
@@ -122,11 +127,10 @@
     share = weight_ref.shape[0] // gathered_ref.shape[0]
     stats = jnp.zeros((STATS, LANES), jnp.float32)
     for place in range(gathered_ref.shape[0]):
-        tile = gathered_ref[place].astype(jnp.float32)
         start = natural(place, sizes) * share
         rows_ref[start : start + 64, :] = gathered_ref[place]
-        rows_ref[start + 64 : start + share, :] = turned(tile[:48]).astype(jnp.bfloat16)
-        stats = stats + tile[48:]
+        rows_ref[start + 64 : start + share, :] = exchanged(gathered_ref[place, :48])
+        stats = stats + gathered_ref[place, 48:].astype(jnp.float32)
     stats = turned(stats[:8] + stats[8:])
     inverse = lax.rsqrt(stats[0:1] / width + EPSILON)
     projected = lax.dot_general(
@@ -159,9 +163,7 @@
     for place in range(gathered_ref.shape[0]):
         start = natural(place, sizes) * 64
         rows_ref[start : start + 32, :] = gathered_ref[place]
-        rows_ref[start + 32 : start + 64, :] = turned(
-            gathered_ref[place].astype(jnp.float32)
-        ).astype(jnp.bfloat16)
+        rows_ref[start + 32 : start + 64, :] = exchanged(gathered_ref[place])
     return state_ref[...] + jnp.dot(
         weight_ref[...], rows_ref[...], preferred_element_type=jnp.float32
     )

time: 202 us -> 202 us (level)
  no operation moved by 1% of the time
where the time goes in v7:
time: 202 us; the launch traced here: 201 us
  blocking collectives  189 us (94%)
  Pallas kernels  5.64 us (3%)
  starting transfers between devices  4.32 us (2%)
    all_gather x4, blocking collectives, gathered(): column = lax.all_gather(tile, 'zh')  125 us
    all_to_all x4, blocking collectives, gathered(): return lax.all_to_all(copies, PLANE, 0, 0).reshape(-1, *tile.shape)  64.5 us
    pallas_call x6, Pallas kernels, local(): pl.pallas_call(kernel, out_shape=outs, in_specs=[smem] * scalars + [given...  5.64 us
    ppermute x2, starting transfers between devices, passed_along(): return lax.ppermute(block, axis, route)  4.32 us
  transfers between devices with their start and end apart: 2, of which 1 were waited for; matrix products, arithmetic and copies ran while one was open for 0% of the time, Pallas kernels for 0%

profile of v7, /device:TPU:2, one launch (start us, length us, event | category | flops | bytes accessed | tf_op | source)
XLA Modules:
  0.0 201.2 jit_solution(9065602756929916589)
XLA Ops:
  0.6 0.0 copy-start
  0.6 0.0 copy-start.2
  0.7 1.5 shard_map.86
  2.2 43.8 %all-gather = bf16[256,128]{1,0:T(8,128)(2,1)S(1)} all-gather(bf16[64,128]{1,0:T(8,128)(2,1)S(1)} %get-tuple-element.9), channel_id=2, replica_groups=mesh['pipe'=16,'y'=4,'zh'=4,'x'=4] {'zh'}, dimensions={0}, use_global_device_ids=true | all-gather | bytes 81920 | tf_op jit(solution)/shard_map/all_gather | solution.py:23
  46.0 0.2 broadcast_in_dim.12
  46.3 20.2 %all_to_all.20 = bf16[16,4,64,128]{3,2,1,0:T(8,128)(2,1)S(1)} all-to-all(bf16[16,4,64,128]{3,2,1,0:T(8,128)(2,1)S(1)} %broadcast_in_dim.12), channel_id=1, replica_groups=mesh['pipe'=16,'y'=4,'zh'=4,'x'=4] {'y','x'}, dimensions={0} | all-to-all | bytes 2097152 | tf_op jit(solution)/shard_map/all_to_all | solution.py:25
  66.4 0.0 copy-done
  66.4 0.0 copy-done.2
  66.4 0.0 copy-start.1
  66.5 1.1 shard_map.87
  67.5 26.9 %all-gather.1 = bf16[128,128]{1,0:T(8,128)(2,1)S(1)} all-gather(bf16[32,128]{1,0:T(8,128)(2,1)S(1)} %shard_map.87), channel_id=3, replica_groups=mesh['pipe'=16,'y'=4,'zh'=4,'x'=4] {'zh'}, dimensions={0}, use_global_device_ids=true | all-gather | bytes 40960 | tf_op jit(solution)/shard_map/all_gather | solution.py:23
  94.5 0.1 broadcast_in_dim.13
  94.6 13.0 %all_to_all.21 = bf16[16,4,32,128]{3,2,1,0:T(8,128)(2,1)S(1)} all-to-all(bf16[16,4,32,128]{3,2,1,0:T(8,128)(2,1)S(1)} %broadcast_in_dim.13), channel_id=1, replica_groups=mesh['pipe'=16,'y'=4,'zh'=4,'x'=4] {'y','x'}, dimensions={0} | all-to-all | bytes 1048576 | tf_op jit(solution)/shard_map/all_to_all | solution.py:25
  107.6 0.0 copy-done.1
  107.6 0.6 shard_map.88
  108.1 1.3 collective-permute-start.1
  109.4 3.0 %collective-permute-start = (bf16[64,128]{1,0:T(8,128)(2,1)S(1)}, bf16[64,128]{1,0:T(8,128)(2,1)S(1)}, u32[]{:S(2)}, u32[]{:S(2)}) collective-permute-start(bf16[64,128]{1,0:T(8,128)(2,1)S(1)} %shard_map.88), channel_id=1, source_target_pairs={{0,64},{64,128},{128,192},{192,256},{256,320},{320,384},{384,448},... | collective-permute-start | bytes 49160 | tf_op jit(solution)/shard_map/ppermute | solution.py:19
  112.5 0.0 collective-permute-done.1.next_ref
  112.5 0.8 collective-permute-done.previous_ref
  113.3 0.2 shard_map.89
  113.5 26.9 %all-gather.2 = bf16[256,128]{1,0:T(8,128)(2,1)S(1)} all-gather(bf16[64,128]{1,0:T(8,128)(2,1)S(1)} %get-tuple-element.12), channel_id=4, replica_groups=mesh['pipe'=16,'y'=4,'zh'=4,'x'=4] {'zh'}, dimensions={0}, use_global_device_ids=true | all-gather | bytes 81920 | tf_op jit(solution)/shard_map/all_gather | solution.py:23
  140.5 0.2 broadcast_in_dim.14
  140.7 18.3 %all_to_all.22 = bf16[16,4,64,128]{3,2,1,0:T(8,128)(2,1)S(1)} all-to-all(bf16[16,4,64,128]{3,2,1,0:T(8,128)(2,1)S(1)} %broadcast_in_dim.14), channel_id=1, replica_groups=mesh['pipe'=16,'y'=4,'zh'=4,'x'=4] {'y','x'}, dimensions={0} | all-to-all | bytes 2097152 | tf_op jit(solution)/shard_map/all_to_all | solution.py:25
  159.0 1.1 shard_map.90
  160.1 26.9 %all-gather.3 = bf16[128,128]{1,0:T(8,128)(2,1)S(1)} all-gather(bf16[32,128]{1,0:T(8,128)(2,1)S(1)} %shard_map.90), channel_id=5, replica_groups=mesh['pipe'=16,'y'=4,'zh'=4,'x'=4] {'zh'}, dimensions={0}, use_global_device_ids=true | all-gather | bytes 40960 | tf_op jit(solution)/shard_map/all_gather | solution.py:23
  187.0 0.1 broadcast_in_dim.15
  187.1 13.0 %all_to_all.23 = bf16[16,4,32,128]{3,2,1,0:T(8,128)(2,1)S(1)} all-to-all(bf16[16,4,32,128]{3,2,1,0:T(8,128)(2,1)S(1)} %broadcast_in_dim.15), channel_id=1, replica_groups=mesh['pipe'=16,'y'=4,'zh'=4,'x'=4] {'y','x'}, dimensions={0} | all-to-all | bytes 1048576 | tf_op jit(solution)/shard_map/all_to_all | solution.py:25
  200.1 1.1 shard_map.91
Async XLA Ops:
  0.6 65.8 %copy-start = (bf16[1,7168,128]{2,1,0:T(8,128)(2,1)S(1)}, bf16[1,7168,128]{2,1,0:T(8,128)(2,1)}, u32[]{:S(2)}) copy-start(bf16[1,7168,128]{2,1,0:T(8,128)(2,1)} %param.12) | copy-start | bytes 5505028
  0.6 65.8 %copy-start.2 = (s32[2,2,1,32,2]{3,4,2,1,0:T(2,128)S(1)}, s32[2,2,1,32,2]{3,4,2,1,0:T(2,128)}, u32[]{:S(2)}) copy-start(s32[2,2,1,32,2]{3,4,2,1,0:T(2,128)} %param.9) | copy-start | bytes 3076
  66.4 41.1 %copy-start.1 = (bf16[1,4096,112]{1,2,0:T(8,128)(2,1)S(1)}, bf16[1,4096,112]{1,2,0:T(8,128)(2,1)}, u32[]{:S(2)}) copy-start(bf16[1,4096,112]{1,2,0:T(8,128)(2,1)} %param.13) | copy-start | bytes 2752516
  108.1 4.3 %collective-permute-start.1 = (bf16[64,128]{1,0:T(8,128)(2,1)S(1)}, bf16[64,128]{1,0:T(8,128)(2,1)S(1)}, u32[]{:S(2)}, u32[]{:S(2)}) collective-permute-start(bf16[64,128]{1,0:T(8,128)(2,1)S(1)} %shard_map.88), channel_id=1, source_target_pairs={{64,0},{128,64},{192,128},{256,192},{320,256},{384,320},{448,384},... | collective-permute-start | bytes 49160 | tf_op jit(solution)/shard_map/ppermute | solution.py:19
  109.4 3.9 %collective-permute-start = (bf16[64,128]{1,0:T(8,128)(2,1)S(1)}, bf16[64,128]{1,0:T(8,128)(2,1)S(1)}, u32[]{:S(2)}, u32[]{:S(2)}) collective-permute-start(bf16[64,128]{1,0:T(8,128)(2,1)S(1)} %shard_map.88), channel_id=1, source_target_pairs={{0,64},{64,128},{128,192},{192,256},{256,320},{320,384},{384,448},... | collective-permute-start | bytes 49160 | tf_op jit(solution)/shard_map/ppermute | solution.py:19

commit v8 on v7

--- a/solution.py
+++ b/solution.py
@@ -13,9 +13,9 @@
 STATS = 16
 
 
-def passed_along(block, axis, distance):
-    devices = range(lax.axis_size(axis))
-    route = [(i - distance, i) for i in devices if i - distance in devices]
+def swapped(block, axis, first):
+    lower = range(first, lax.axis_size(axis) - 1, 2)
+    route = [(i, i + 1) for i in lower] + [(i + 1, i) for i in lower]
     return lax.ppermute(block, axis, route)
 
 
@@ -108,12 +108,13 @@
     write_tile(rows, coefs, tile_ref)
 
 
-def pass_kernel(previous_ref, next_ref, coefs_ref, tile_ref, state_ref):
+def pass_kernel(section_ref, even_ref, odd_ref, coefs_ref, tile_ref, state_ref):
     lane = lax.broadcasted_iota(jnp.int32, (64, LANES), 1)
+    forward = (lane % 64 < 32).astype(jnp.int32)
     mixed = jnp.where(
-        lane % 64 < 32,
-        previous_ref[...].astype(jnp.float32),
-        next_ref[...].astype(jnp.float32),
+        forward == lax.rem(section_ref[0], 2),
+        even_ref[...].astype(jnp.float32),
+        odd_ref[...].astype(jnp.float32),
     )
     rows = jnp.concatenate([mixed, turned(mixed)[:48]], axis=0)
     state_ref[...] = rows
@@ -266,9 +267,11 @@
                 entry_outs,
                 [],
                 0,
-                passed_along(raw, "pipe", 1),
-                passed_along(raw, "pipe", -1),
+                lax.axis_index("pipe").reshape(1),
+                swapped(raw, "pipe", 0),
+                swapped(raw, "pipe", 1),
                 coefs,
+                scalars=1,
             )
         else:
             rows_out = jax.ShapeDtypeStruct((forward_rows.shape[1], share), half)

time: 202 us -> 202 us (level)
  no operation moved by 1% of the time
where the time goes in v8:
time: 202 us
  blocking collectives  189 us (94%)
  Pallas kernels  5.63 us (3%)
  starting transfers between devices  5.05 us (2%)
    all_gather x4, blocking collectives, gathered(): column = lax.all_gather(tile, 'zh')  125 us
    all_to_all x4, blocking collectives, gathered(): return lax.all_to_all(copies, PLANE, 0, 0).reshape(-1, *tile.shape)  63.9 us
    pallas_call x6, Pallas kernels, local(): pl.pallas_call(kernel, out_shape=outs, in_specs=[smem] * scalars + [given...  5.63 us
    ppermute x2, starting transfers between devices, swapped(): return lax.ppermute(block, axis, route)  5.05 us
  transfers between devices with their start and end apart: 2, of which 1 were waited for; matrix products, arithmetic and copies ran while one was open for 0% of the time, Pallas kernels for 0%

profile of v8, /device:TPU:2, one launch (start us, length us, event | category | flops | bytes accessed | tf_op | source)
XLA Modules:
  0.0 201.5 jit_solution(18289218184009906227)
XLA Ops:
  0.6 0.0 copy-start
  0.6 0.0 copy-start.2
  0.7 1.5 shard_map.86
  2.2 43.8 %all-gather = bf16[256,128]{1,0:T(8,128)(2,1)S(1)} all-gather(bf16[64,128]{1,0:T(8,128)(2,1)S(1)} %get-tuple-element.9), channel_id=2, replica_groups=mesh['pipe'=16,'y'=4,'zh'=4,'x'=4] {'zh'}, dimensions={0}, use_global_device_ids=true | all-gather | bytes 81920 | tf_op jit(solution)/shard_map/all_gather | solution.py:23
  46.0 0.2 broadcast_in_dim.12
  46.3 20.2 %all_to_all.20 = bf16[16,4,64,128]{3,2,1,0:T(8,128)(2,1)S(1)} all-to-all(bf16[16,4,64,128]{3,2,1,0:T(8,128)(2,1)S(1)} %broadcast_in_dim.12), channel_id=1, replica_groups=mesh['pipe'=16,'y'=4,'zh'=4,'x'=4] {'y','x'}, dimensions={0} | all-to-all | bytes 2097152 | tf_op jit(solution)/shard_map/all_to_all | solution.py:25
  66.4 0.0 copy-done
  66.4 0.0 copy-done.2
  66.4 0.0 copy-start.1
  66.5 1.1 shard_map.87
  67.5 26.9 %all-gather.1 = bf16[128,128]{1,0:T(8,128)(2,1)S(1)} all-gather(bf16[32,128]{1,0:T(8,128)(2,1)S(1)} %shard_map.87), channel_id=3, replica_groups=mesh['pipe'=16,'y'=4,'zh'=4,'x'=4] {'zh'}, dimensions={0}, use_global_device_ids=true | all-gather | bytes 40960 | tf_op jit(solution)/shard_map/all_gather | solution.py:23
  94.5 0.1 broadcast_in_dim.13
  94.6 13.0 %all_to_all.21 = bf16[16,4,32,128]{3,2,1,0:T(8,128)(2,1)S(1)} all-to-all(bf16[16,4,32,128]{3,2,1,0:T(8,128)(2,1)S(1)} %broadcast_in_dim.13), channel_id=1, replica_groups=mesh['pipe'=16,'y'=4,'zh'=4,'x'=4] {'y','x'}, dimensions={0} | all-to-all | bytes 1048576 | tf_op jit(solution)/shard_map/all_to_all | solution.py:25
  107.6 0.0 copy-done.1
  107.6 0.6 shard_map.88
  108.1 0.7 collective-permute-start.1
  108.8 4.4 %collective-permute-start = (bf16[64,128]{1,0:T(8,128)(2,1)S(1)}, bf16[64,128]{1,0:T(8,128)(2,1)S(1)}, u32[]{:S(2)}, u32[]{:S(2)}) collective-permute-start(bf16[64,128]{1,0:T(8,128)(2,1)S(1)} %shard_map.88), channel_id=1, source_target_pairs={{0,64},{128,192},{256,320},{384,448},{512,576},{640,704},{768,832}... | collective-permute-start | bytes 49160 | tf_op jit(solution)/shard_map/ppermute | solution.py:19
  113.2 0.0 collective-permute-done.1.odd_ref
  113.2 0.8 collective-permute-done.even_ref
  114.0 0.2 shard_map.89
  114.3 27.1 %all-gather.2 = bf16[256,128]{1,0:T(8,128)(2,1)S(1)} all-gather(bf16[64,128]{1,0:T(8,128)(2,1)S(1)} %get-tuple-element.12), channel_id=4, replica_groups=mesh['pipe'=16,'y'=4,'zh'=4,'x'=4] {'zh'}, dimensions={0}, use_global_device_ids=true | all-gather | bytes 81920 | tf_op jit(solution)/shard_map/all_gather | solution.py:23
  141.4 0.2 broadcast_in_dim.14
  141.6 17.6 %all_to_all.22 = bf16[16,4,64,128]{3,2,1,0:T(8,128)(2,1)S(1)} all-to-all(bf16[16,4,64,128]{3,2,1,0:T(8,128)(2,1)S(1)} %broadcast_in_dim.14), channel_id=1, replica_groups=mesh['pipe'=16,'y'=4,'zh'=4,'x'=4] {'y','x'}, dimensions={0} | all-to-all | bytes 2097152 | tf_op jit(solution)/shard_map/all_to_all | solution.py:25
  159.3 1.1 shard_map.90
  160.4 26.9 %all-gather.3 = bf16[128,128]{1,0:T(8,128)(2,1)S(1)} all-gather(bf16[32,128]{1,0:T(8,128)(2,1)S(1)} %shard_map.90), channel_id=5, replica_groups=mesh['pipe'=16,'y'=4,'zh'=4,'x'=4] {'zh'}, dimensions={0}, use_global_device_ids=true | all-gather | bytes 40960 | tf_op jit(solution)/shard_map/all_gather | solution.py:23
  187.3 0.1 broadcast_in_dim.15
  187.4 13.0 %all_to_all.23 = bf16[16,4,32,128]{3,2,1,0:T(8,128)(2,1)S(1)} all-to-all(bf16[16,4,32,128]{3,2,1,0:T(8,128)(2,1)S(1)} %broadcast_in_dim.15), channel_id=1, replica_groups=mesh['pipe'=16,'y'=4,'zh'=4,'x'=4] {'y','x'}, dimensions={0} | all-to-all | bytes 1048576 | tf_op jit(solution)/shard_map/all_to_all | solution.py:25
  200.4 1.1 shard_map.91
Async XLA Ops:
  0.6 65.8 %copy-start = (bf16[1,7168,128]{2,1,0:T(8,128)(2,1)S(1)}, bf16[1,7168,128]{2,1,0:T(8,128)(2,1)}, u32[]{:S(2)}) copy-start(bf16[1,7168,128]{2,1,0:T(8,128)(2,1)} %param.12) | copy-start | bytes 5505028
  0.6 65.8 %copy-start.2 = (s32[2,2,1,32,2]{3,4,2,1,0:T(2,128)S(1)}, s32[2,2,1,32,2]{3,4,2,1,0:T(2,128)}, u32[]{:S(2)}) copy-start(s32[2,2,1,32,2]{3,4,2,1,0:T(2,128)} %param.9) | copy-start | bytes 3076
  66.4 41.1 %copy-start.1 = (bf16[1,4096,112]{1,2,0:T(8,128)(2,1)S(1)}, bf16[1,4096,112]{1,2,0:T(8,128)(2,1)}, u32[]{:S(2)}) copy-start(bf16[1,4096,112]{1,2,0:T(8,128)(2,1)} %param.13) | copy-start | bytes 2752516
  108.1 5.1 %collective-permute-start.1 = (bf16[64,128]{1,0:T(8,128)(2,1)S(1)}, bf16[64,128]{1,0:T(8,128)(2,1)S(1)}, u32[]{:S(2)}, u32[]{:S(2)}) collective-permute-start(bf16[64,128]{1,0:T(8,128)(2,1)S(1)} %shard_map.88), channel_id=1, source_target_pairs={{64,128},{192,256},{320,384},{448,512},{576,640},{704,768},{832,89... | collective-permute-start | bytes 49160 | tf_op jit(solution)/shard_map/ppermute | solution.py:19
  108.8 5.2 %collective-permute-start = (bf16[64,128]{1,0:T(8,128)(2,1)S(1)}, bf16[64,128]{1,0:T(8,128)(2,1)S(1)}, u32[]{:S(2)}, u32[]{:S(2)}) collective-permute-start(bf16[64,128]{1,0:T(8,128)(2,1)S(1)} %shard_map.88), channel_id=1, source_target_pairs={{0,64},{128,192},{256,320},{384,448},{512,576},{640,704},{768,832}... | collective-permute-start | bytes 49160 | tf_op jit(solution)/shard_map/ppermute | solution.py:19
